TPU v7x, 32 devices: a whole 2x2x4 slice. The times are simulated.
32 devices in a mesh: groups: 2 (over x), blk: 16 (over z, y, core).
Axes of the slice: x: 2, y: 2, z: 4, core: 2. Of those that a mesh axis runs over, the one named last changes fastest.
Arguments:
- train_in: bfloat16 [32, 4096], P(('groups', 'blk')), parts along dimension 0, may hold values from -0.09375 to 0.09375
- train_out: bfloat16 [32, 14336], P(('groups', 'blk')), parts along dimension 0, may hold values from -0.050048828 to 0.050048828
- query_in: bfloat16 [64, 4096], P('groups'), parts along dimension 0, may hold values from -6 to 6
- query_out: bfloat16 [64, 14336], P('groups'), parts along dimension 0, may hold values from -6 to 6
- basis_in: bfloat16 [8192, 4096], P(('groups', 'blk')), parts along dimension 0, may hold values from -0.09375 to 0.09375
- basis_out: bfloat16 [28672, 14336], P(('groups', 'blk')), parts along dimension 0, may hold values from -0.046875 to 0.046875
- eigvals: float32 [28672, 4096], P(('groups', 'blk')), parts along dimension 0, may hold values from 0.05 to 18, as said below
Outputs:
- scores: float32 [32, 32], P(('groups', 'blk')), parts along dimension 0
There are 2 independent parts, one for each index of `groups`. A program takes and returns all parts, laid end to end along the dimension named above; each array names one. Nothing has to cross between parts.
Inputs may be any that keep to these rules, and one draw needn't show every extreme that they name: `eigvals`: eigenvalue corrections, all positive.
All inputs are finite; a program needn't handle non-finite values.
Results may differ from a plain program's by a relative error of at most 0.006.
Values may be sent and summed in bfloat16 or wider, within the bound.
No kernel may reach another device: no remote copies, remote signals or barrier semaphores. Data moves between devices by JAX's collectives and lax.ppermute only.
A program may use at most 128 MiB of HBM per device.

v0:
```python
import math

import jax
import jax.numpy as jnp
from jax import lax
from jax.sharding import PartitionSpec as P

D_IN = 4096
D_OUT = 14336


def shards(train_in, train_out, query_in, query_out, basis_in, basis_out, eigvals):
    contract = (((1,), (1,)), ((), ()))
    local_total = jnp.sum(eigvals)
    grand_total = lax.psum(local_total, "blk")
    damping = 0.1 * grand_total / (D_OUT * D_IN)
    inverse = (1.0 / (eigvals + damping)).astype(jnp.bfloat16)

    def rotate_out(piece):
        return lax.dot_general(
            piece, basis_out, contract, preferred_element_type=jnp.float32
        ).astype(jnp.bfloat16)

    all_in = lax.all_gather(train_in, "blk", axis=0, tiled=True)
    out_train = rotate_out(lax.all_gather(train_out, "blk", axis=0, tiled=True))
    out_query = rotate_out(query_out)
    stacked = jnp.concatenate([all_in, query_in], axis=0)
    own_part = lax.dot_general(
        stacked, basis_in, contract, preferred_element_type=jnp.float32
    ).astype(jnp.bfloat16)
    rotated = lax.all_gather(own_part, "blk", axis=1, tiled=True)
    count_train = all_in.shape[0]
    in_train = rotated[:count_train]
    in_query = rotated[count_train:]
    query_count = in_query.shape[0]
    width_in = in_query.shape[1]
    query_weight = out_query.astype(jnp.float32)
    block = math.gcd(count_train, max(8, 512 // query_count))
    steps = count_train // block

    def one_block(index, result):
        first = index * block
        rows_block = lax.dynamic_slice_in_dim(in_train, first, block, 0)
        weight_block = lax.dynamic_slice_in_dim(out_train, first, block, 0).astype(jnp.float32)
        pair = rows_block[:, None, :] * in_query[None, :, :]
        damped = lax.dot_general(
            pair.reshape(block * query_count, width_in),
            inverse,
            contract,
            preferred_element_type=jnp.float32,
        )
        damped = damped.reshape(block, query_count, -1)
        weight = weight_block[:, None, :] * query_weight[None, :, :]
        summed = jnp.sum(damped * weight, axis=2)
        return lax.dynamic_update_slice_in_dim(result, summed, first, 0)

    initial = jnp.zeros((count_train, query_count), jnp.float32)
    all_terms = lax.fori_loop(0, steps, one_block, initial)
    return lax.psum_scatter(all_terms, "blk", scatter_dimension=0, tiled=True)


def solution(mesh):
    in_specs = (
        P(("groups", "blk"), None),
        P(("groups", "blk"), None),
        P("groups", None),
        P("groups", None),
        P(("groups", "blk"), None),
        P(("groups", "blk"), None),
        P(("groups", "blk"), None),
    )
    out_specs = P(("groups", "blk"), None)
    return jax.shard_map(shards, mesh=mesh, in_specs=in_specs, out_specs=out_specs, check_vma=False)
```

profile of v0, /device:TPU:0, one launch (start us, length us, event | category | flops | bytes accessed | tf_op | source)
XLA Modules:
  0.0 175.1 jit_solution(18043039171966553123)
XLA Ops:
  0.0 0.0 copy-start
  0.0 24.2 %all-gather = bf16[16,1,4096]{2,1,0:T(2,128)(2,1)S(1)} all-gather(bf16[1,1,4096]{2,1,0:T(2,128)(2,1)} %bitcast.20), channel_id=1, replica_groups=mesh['groups'=2,'blk'=16] {'blk'}, dimensions={0}, use_global_device_ids=true | all-gather | bytes 139264 | tf_op jit(solution)/shard_map/all_gather | solution.py:24
  24.2 0.1 copy.15
  24.3 0.0 copy-done
  24.3 1.7 convolution_convert_fusion.2
  26.0 18.5 %all_gather.10 = bf16[48,4096]{1,0:T(8,128)(2,1)S(1)} all-gather(bf16[48,256]{1,0:T(8,128)(2,1)S(1)} %convolution_convert_fusion.2), channel_id=1, replica_groups=mesh['groups'=2,'blk'=16] {'blk'}, dimensions={1}, use_global_device_ids=true | all-gather | bytes 417792 | tf_op jit(solution)/shard_map/all_gather | solution.py:31
  44.5 0.0 copy-start.1
  44.5 21.6 %all-gather.1 = bf16[16,1,14336]{2,1,0:T(2,128)(2,1)S(1)} all-gather(bf16[1,1,14336]{2,1,0:T(2,128)(2,1)} %bitcast.19), channel_id=1, replica_groups=mesh['groups'=2,'blk'=16] {'blk'}, dimensions={0}, use_global_device_ids=true | all-gather | bytes 487424 | tf_op jit(solution)/shard_map/all_gather | solution.py:25
  66.2 11.7 %fusion.10 = f32[16,896]{1,0:T(8,128)S(1)} fusion(bf16[896,14336]{1,0:T(8,128)(2,1)} %param.12, bf16[16,1,14336]{2,1,0:T(2,128)(2,1)S(1)} %all-gather.1), kind=kOutput, calls=%fused_computation.10 | convolution fusion | flops 411070464 | bytes 26206208 | tf_op jit(solution)/shard_map/dot_general | solution.py:20
  77.9 0.0 copy-done.1
  77.9 14.6 %fusion.9 = f32[32,896]{1,0:T(8,128)S(1)} fusion(bf16[32,14336]{1,0:T(8,128)(2,1)} %param.10, bf16[896,14336]{1,0:T(8,128)(2,1)} %param.12), kind=kOutput, calls=%fused_computation.8 | convolution fusion | flops 822140928 | bytes 26722304 | tf_op jit(solution)/shard_map/dot_general | solution.py:20
  92.5 0.0 slice-start
  92.5 0.0 slice-start.1
  92.5 9.6 %reduce_sum.19 = f32[]{:T(128)} reduce(f32[896,4096]{1,0:T(8,128)} %param.13, f32[]{:T(128)} %constant.8.clone.1), dimensions={0,1}, to_apply=%region_0.0 | reduce | flops 3670015 | bytes 14680072 | tf_op jit(solution)/shard_map/reduce_sum | solution.py:14
  102.1 30.6 %psum.7 = f32[]{:T(128)} all-reduce(f32[]{:T(128)} %reduce_sum.19), channel_id=1, replica_groups=mesh['groups'=2,'blk'=16] {'blk'}, use_global_device_ids=true, to_apply=%region_1.0 | all-reduce | flops 1 | bytes 8 | tf_op jit(solution)/shard_map/psum | solution.py:15
  133.4 0.0 slice-done
  133.4 0.0 slice-done.1
  133.4 0.0 copy-start.2
  133.4 9.8 %multiply_reduce_fusion = f32[16,32]{1,0:T(8,128)S(1)} fusion(f32[896,4096]{1,0:T(8,128)} %param.13, f32[]{:T(128)S(6)} %div.10, bf16[32,4096]{1,0:T(8,128)(2,1)S(1)} %slice-done, bf16[16,4096]{1,0:T(8,128)(2,1)S(1)} %slice-done.1, f32[32,896]{1,0:T(8,128)S(1)} %fusion.9, f32[16,896]{1,0:T(8,128)S(1)} %fusion.10), kind=kOutput, calls=%fused_computation.6 | convolution fusion | flops 3772579328 | bytes 15247364 | tf_op jit(solution)/shard_map/while/body/eval_jaxpr/dot_general | solution.py:46
  143.2 30.0 %all-reduce = f32[16,32]{1,0:T(8,128)S(1)} all-reduce(f32[16,32]{1,0:T(8,128)S(1)} %multiply_reduce_fusion), channel_id=2, replica_groups=mesh['groups'=2,'blk'=16] {'blk'}, use_global_device_ids=true, to_apply=%region_3.4.clone | all-reduce | flops 512 | bytes 4096
  173.2 0.0 copy-done.2
  173.2 0.7 dynamic-slice
  173.9 1.2 constant_dynamic-slice_fusion
Async XLA Ops:
  0.0 24.3 %copy-start = (bf16[256,4096]{1,0:T(8,128)(2,1)S(1)}, bf16[256,4096]{1,0:T(8,128)(2,1)}, u32[]{:S(2)}) copy-start(bf16[256,4096]{1,0:T(8,128)(2,1)} %param.11) | copy-start | bytes 6291460
  44.5 33.4 %copy-start.1 = (bf16[48,4096]{1,0:T(8,128)(2,1)}, bf16[48,4096]{1,0:T(8,128)(2,1)S(1)}, u32[]{:S(2)}) copy-start(bf16[48,4096]{1,0:T(8,128)(2,1)S(1)} %all_gather.10) | copy-start | bytes 1179652
  92.5 40.9 %slice-start = ((bf16[48,4096]{1,0:T(8,128)(2,1)}), bf16[32,4096]{1,0:T(8,128)(2,1)S(1)}, s32[]{:S(2)}) async-start(bf16[48,4096]{1,0:T(8,128)(2,1)} %copy-done.1), calls=%async_computation | async-start | bytes 524288 | tf_op jit(solution)/shard_map/slice | solution.py:34
  92.5 40.9 %slice-start.1 = ((bf16[48,4096]{1,0:T(8,128)(2,1)}), bf16[16,4096]{1,0:T(8,128)(2,1)S(1)}, s32[]{:S(2)}) async-start(bf16[48,4096]{1,0:T(8,128)(2,1)} %copy-done.1), calls=%async_computation.1 | async-start | bytes 262144 | tf_op jit(solution)/shard_map/slice | solution.py:33
  133.4 39.8 %copy-start.2 = (u32[32]{0:T(128)S(1)}, u32[32]{0:T(128)}, u32[]{:S(2)}) copy-start(u32[32]{0:T(128)} %constant.25) | copy-start | bytes 388
where the time goes:
time: 175 us
  blocking collectives  125 us (71%)
  matrix products  37.8 us (22%)
  other arithmetic  9.6 us (5%)
  local copies, waits for them, and re-layouts  2.04 us (1%)
    psum x1, blocking collectives, shards(): grand_total = lax.psum(local_total, 'blk')  30.6 us
    unnamed x1, blocking collectives  30 us
    dot_general x2, matrix products, rotate_out(): lax.dot_general(piece, basis_out, contract, preferred_element_type=jnp.fl...  26.3 us
    all_gather x1, blocking collectives, shards(): all_in = lax.all_gather(train_in, 'blk', axis=0, tiled=True)  24.2 us
    all_gather x1, blocking collectives, shards(): out_train = rotate_out(lax.all_gather(train_out, 'blk', axis=0, tiled=True))  21.6 us
    all_gather x1, blocking collectives, shards(): rotated = lax.all_gather(own_part, 'blk', axis=1, tiled=True)  18.5 us
    dot_general x1, matrix products, one_block(): lax.dot_general(pair.reshape(block * query_count, width_in), inverse, con...  9.79 us
    reduce_sum x1, other arithmetic, shards(): local_total = jnp.sum(eigvals)  9.6 us

commit v1 on v0

v1 whole, which is shorter than its diff:
```python
import jax
import jax.numpy as jnp
from jax import lax
from jax.sharding import PartitionSpec as P

CONTRACT = (((1,), (1,)), ((), ()))


def stage_bits(count):
    bits = [1 << k for k in range(count.bit_length() - 1)]
    return bits[1:] + bits[:1]


def swap(piece, bit, count):
    return lax.ppermute(piece, "blk", [(i, i ^ bit) for i in range(count)])


def slot_order(count):
    order = [0]
    for bit in stage_bits(count):
        order = order + [j ^ bit for j in order]
    return order


def gather_slots(piece, count):
    for bit in stage_bits(count):
        piece = jnp.concatenate([piece, swap(piece, bit, count)], axis=0)
    return piece


def scatter_slots(piece, count):
    for bit in reversed(stage_bits(count)):
        half = piece.shape[0] // 2
        piece = piece[:half] + swap(piece[half:], bit, count)
    return piece


def dot(left, right):
    return lax.dot_general(left, right, CONTRACT, preferred_element_type=jnp.float32)


def split_sum(total):
    high = lax.reduce_precision(total, 8, 7)
    middle = lax.reduce_precision(total - high, 8, 7)
    low = total - high - middle
    return jnp.stack([high, middle, low]).astype(jnp.bfloat16)


def make_shards(count, d_in, d_out):
    def shards(train_in, train_out, query_in, query_out, basis_in, basis_out, eigvals):
        me = lax.axis_index("blk")
        order = jnp.asarray(slot_order(count), jnp.int32)
        local_train = train_in.shape[0]
        queries = query_in.shape[0]
        width = basis_in.shape[0]
        n_train = local_train * count

        sums = jnp.broadcast_to(split_sum(jnp.sum(eigvals))[:, None], (3, width))
        query_part = dot(query_in, basis_in).astype(jnp.bfloat16)
        out_query = dot(query_out, basis_out).astype(jnp.bfloat16)
        all_in = gather_slots(train_in, count)
        train_part = dot(all_in, basis_in).astype(jnp.bfloat16)
        train_part = train_part.reshape(count, local_train, width)
        train_part = jnp.take(train_part, jnp.argsort(order)[me ^ jnp.arange(count)], axis=0).reshape(n_train, width)
        parts = jnp.concatenate([train_part, query_part, sums], axis=0)
        gathered = gather_slots(parts[None], count)
        gathered = jnp.take(gathered, jnp.argsort(order)[me ^ jnp.arange(count)], axis=0)
        total = jnp.sum(gathered[:, n_train + queries :, 0].astype(jnp.float32))
        rotated = jnp.transpose(gathered[:, : n_train + queries], (1, 0, 2)).reshape(n_train + queries, -1)
        damping = 0.1 * total / (d_out * d_in)
        inverse = (1.0 / (eigvals + damping)).astype(jnp.bfloat16)

        all_out = gather_slots(train_out, count).reshape(count, local_train, -1)
        out_train = dot(all_out.reshape(n_train, -1), basis_out).astype(jnp.bfloat16)

        in_train = rotated[:n_train].reshape(count, local_train, -1)
        in_train = jnp.take(in_train, me ^ order, axis=0).reshape(n_train, -1)
        in_query = rotated[n_train:]
        pair = in_train[:, None, :] * in_query[None, :, :]
        damped = dot(pair.reshape(n_train * queries, -1), inverse).reshape(n_train, queries, -1)
        weight = out_train.astype(jnp.float32)[:, None, :] * out_query.astype(jnp.float32)[None, :, :]
        terms = jnp.sum(damped * weight, axis=2)
        return scatter_slots(terms, count)

    return shards


def solution(mesh):
    in_specs = (
        P(("groups", "blk"), None),
        P(("groups", "blk"), None),
        P("groups", None),
        P("groups", None),
        P(("groups", "blk"), None),
        P(("groups", "blk"), None),
        P(("groups", "blk"), None),
    )
    out_specs = P(("groups", "blk"), None)
    count = mesh.shape["blk"]

    def run(train_in, train_out, query_in, query_out, basis_in, basis_out, eigvals):
        shards = make_shards(count, train_in.shape[1], train_out.shape[1])
        return jax.shard_map(shards, mesh=mesh, in_specs=in_specs, out_specs=out_specs, check_vma=False)(
            train_in, train_out, query_in, query_out, basis_in, basis_out, eigvals
        )

    return run
```

time: 175 us -> 102 us (0.58)
  blocking collectives: 125 us -> 0 us
  starting transfers between devices: 0 us -> 23.1 us
  waiting for transfers between devices: 0 us -> 18.2 us
  between operations: 0.75 us -> 5.83 us
  local copies, waits for them, and re-layouts: 2.04 us -> 5.68 us
  other arithmetic: 9.6 us -> 12.7 us
    all_gather x3 -> x0, blocking collectives: 64.3 us -> none  [the longest x1 24.2 us: shards(): all_in = lax.all_gather(train_in, 'blk', axis=0, tiled=True)]
    psum x1 -> x0, blocking collectives: 30.6 us -> none  [shards(): grand_total = lax.psum(local_total, 'blk')]
    unnamed x1 -> x0, blocking collectives: 30 us -> none
    ppermute x0 -> x16, starting transfers between devices: none -> 23.1 us  [swap(): return lax.ppermute(piece, 'blk', [(i, i ^ bit) for i in range(count)])]
    ppermute x0 -> x16, waiting for transfers between devices: none -> 18.2 us  [swap(): return lax.ppermute(piece, 'blk', [(i, i ^ bit) for i in range(count)])]
    gather x0 -> x4, local copies, waits for them, and re-layouts: none -> 3.13 us  [the longest x1 1.32 us: shards(): jnp.argsort(order)[me ^ jnp.arange(count)]]
    concatenate x0 -> x3, local copies, waits for them, and re-layouts: none -> 2.4 us  [gather_slots(): piece = jnp.concatenate([piece, swap(piece, bit, count)], axis=0)]
    unnamed x9 -> x15, local copies, waits for them, and re-layouts: 2.03 us -> 0.07 us
  transfers between devices with their start and end apart: 0 -> 16, of which waited for: 0 -> 10; matrix products, arithmetic and copies ran while one was open for 0% -> 40% of each run, Pallas kernels for 0% -> 0%
where the time goes in v1:
time: 102 us
  matrix products  36.2 us (35%)
  starting transfers between devices  23.1 us (23%)
  waiting for transfers between devices  18.2 us (18%)
  other arithmetic  12.7 us (12%)
  between operations  5.83 us (6%)
  local copies, waits for them, and re-layouts  5.68 us (6%)
    dot_general x5, matrix products, dot(): lax.dot_general(left, right, CONTRACT, preferred_element_type=jnp.float32)  36.2 us
    ppermute x16, starting transfers between devices, swap(): return lax.ppermute(piece, 'blk', [(i, i ^ bit) for i in range(count)])  23.1 us
    ppermute x16, waiting for transfers between devices, swap(): return lax.ppermute(piece, 'blk', [(i, i ^ bit) for i in range(count)])  18.2 us
    reduce_sum x1, other arithmetic, shards(): sums = jnp.broadcast_to(split_sum(jnp.sum(eigvals))[:, None], (3, width))  9.57 us
    concatenate x3, local copies, waits for them, and re-layouts, gather_slots(): piece = jnp.concatenate([piece, swap(piece, bit, count)], axis=0)  2.4 us
  transfers between devices with their start and end apart: 16, of which 10 were waited for; matrix products, arithmetic and copies ran while one was open for 40% of the time, Pallas kernels for 0%

profile of v1, /device:TPU:0, one launch (start us, length us, event | category | flops | bytes accessed | tf_op | source)
XLA Modules:
  0.0 101.8 jit_solution(2733423568873348904)
XLA Ops:
  0.0 0.0 copy-start
  0.0 3.0 %collective-permute-start.8 = (bf16[1,14336]{1,0:T(2,128)(2,1)}, bf16[1,14336]{1,0:T(2,128)(2,1)S(1)}, u32[]{:S(2)}, u32[]{:S(2)}) collective-permute-start(bf16[1,14336]{1,0:T(2,128)(2,1)} %param.9), channel_id=1, source_target_pairs={{0,2},{1,3},{2,0},{3,1},{4,6},{5,7},{6,4},{7,5},{8,10},{9,11},{10,... | collective-permute-start | bytes 86024 | tf_op jit(solution)/shard_map/ppermute | solution.py:15
  3.0 0.1 collective-permute-start
  3.0 0.7 compare_and_fusion.1
  3.7 1.3 %gather_fusion = s32[16]{0:T(128)S(1)} fusion(s32[16]{0:T(128)} %constant.61, s32[1024]{0:T(1024)S(1)} %get-tuple-element.10), kind=kCustom, calls=%fused_computation | custom fusion | bytes 192 | tf_op jit(solution)/shard_map/gather | solution.py:67
  5.1 0.0 copy-start.2
  5.1 13.2 %fusion.5 = f32[32,896]{1,0:T(8,128)} fusion(bf16[32,14336]{1,0:T(8,128)(2,1)} %param.11, bf16[896,14336]{1,0:T(8,128)(2,1)} %param.13), kind=kOutput, calls=%fused_computation.12 | convolution fusion | flops 822140928 | bytes 26722304 | tf_op jit(solution)/shard_map/dot_general | solution.py:39
  18.3 0.7 convolution_convert_fusion.2
  19.0 0.0 copy-start.3
  19.0 0.0 copy-start.1
  19.0 9.6 %reduce_sum.27 = f32[]{:T(128)} reduce(f32[896,4096]{1,0:T(8,128)} %param.14, f32[]{:T(128)} %constant.54.clone.1), dimensions={0,1}, to_apply=%region_1.0 | reduce | flops 3670015 | bytes 14680072 | tf_op jit(solution)/shard_map/reduce_sum | solution.py:58
  33.5 0.0 collective-permute-done
  33.6 2.1 %collective-permute-start.1 = (bf16[2,4096]{1,0:T(2,128)(2,1)S(1)}, bf16[2,4096]{1,0:T(2,128)(2,1)S(1)}, u32[]{:S(2)}, u32[]{:S(2)}) collective-permute-start(bf16[2,4096]{1,0:T(2,128)(2,1)S(1)} %pad_maximum_fusion.8), channel_id=1, source_target_pairs={{0,4},{1,5},{2,6},{3,7},{4,0},{5,1},{6,2},{7,3},{8,12},{9,13},{10,... | collective-permute-start | bytes 49160 | tf_op jit(solution)/shard_map/ppermute | solution.py:15
  35.7 0.1 pad_maximum_fusion.9
  35.7 1.6 %collective-permute-done.1 = bf16[2,4096]{1,0:T(2,128)(2,1)S(1)} collective-permute-done((bf16[2,4096]{1,0:T(2,128)(2,1)S(1)}, bf16[2,4096]{1,0:T(2,128)(2,1)S(1)}, u32[]{:S(2)}, u32[]{:S(2)}) %collective-permute-start.1) | collective-permute-done | bytes 16416 | tf_op jit(solution)/shard_map/ppermute | solution.py:15
  37.4 0.1 pad_maximum_fusion.7
  37.5 3.1 %collective-permute-start.2 = (bf16[4,4096]{1,0:T(4,128)(2,1)S(1)}, bf16[4,4096]{1,0:T(4,128)(2,1)S(1)}, u32[]{:S(2)}, u32[]{:S(2)}) collective-permute-start(bf16[4,4096]{1,0:T(4,128)(2,1)S(1)} %pad_maximum_fusion.7), channel_id=1, source_target_pairs={{0,8},{1,9},{2,10},{3,11},{4,12},{5,13},{6,14},{7,15},{8,0},{9,1},... | collective-permute-start | bytes 98312 | tf_op jit(solution)/shard_map/ppermute | solution.py:15
  40.5 0.0 collective-permute-done.8
  40.5 0.0 copy-done.1
  40.5 0.1 pad_maximum_fusion.6
  40.7 1.6 %collective-permute-start.9 = (bf16[2,14336]{1,0:T(2,128)(2,1)S(1)}, bf16[2,14336]{1,0:T(2,128)(2,1)S(1)}, u32[]{:S(2)}, u32[]{:S(2)}) collective-permute-start(bf16[2,14336]{1,0:T(2,128)(2,1)S(1)} %pad_maximum_fusion.6), channel_id=1, source_target_pairs={{0,4},{1,5},{2,6},{3,7},{4,0},{5,1},{6,2},{7,3},{8,12},{9,13},{10,... | collective-permute-start | bytes 172040 | tf_op jit(solution)/shard_map/ppermute | solution.py:15
  42.3 0.1 collective-permute-done.2
  42.4 0.1 pad_maximum_fusion.4
  42.5 0.1 collective-permute-start.3
  42.6 2.3 %collective-permute-done.9 = bf16[2,14336]{1,0:T(2,128)(2,1)S(1)} collective-permute-done((bf16[2,14336]{1,0:T(2,128)(2,1)S(1)}, bf16[2,14336]{1,0:T(2,128)(2,1)S(1)}, u32[]{:S(2)}, u32[]{:S(2)}) %collective-permute-start.9) | collective-permute-done | bytes 57376 | tf_op jit(solution)/shard_map/ppermute | solution.py:15
  44.9 0.2 pad_maximum_fusion.3
  45.1 0.7 collective-permute-start.10
  45.8 0.0 collective-permute-done.3
  45.8 0.1 concatenate.56
  45.9 0.6 convolution_convert_fusion.3
  46.6 0.6 gather_fusion.1
  47.2 0.1 broadcast_select_fusion.2
  47.2 0.1 maximum_bitcast_fusion
  47.3 1.5 %collective-permute-start.4 = (bf16[1,51,256]{2,1,0:T(8,128)(2,1)S(1)}, bf16[1,51,256]{2,1,0:T(8,128)(2,1)S(1)}, u32[]{:S(2)}, u32[]{:S(2)}) collective-permute-start(bf16[1,51,256]{2,1,0:T(8,128)(2,1)S(1)} %maximum_bitcast_fusion), channel_id=1, source_target_pairs={{0,2},{1,3},{2,0},{3,1},{4,6},{5,7},{6,4},{7,5},{8,10},{9,11},{10,... | collective-permute-start | bytes 78344 | tf_op jit(solution)/shard_map/ppermute | solution.py:15
  48.9 0.1 constant_dynamic-update-slice_fusion.4
  48.9 2.3 %collective-permute-done.4 = bf16[1,51,256]{2,1,0:T(8,128)(2,1)S(1)} collective-permute-done((bf16[1,51,256]{2,1,0:T(8,128)(2,1)S(1)}, bf16[1,51,256]{2,1,0:T(8,128)(2,1)S(1)}, u32[]{:S(2)}, u32[]{:S(2)}) %collective-permute-start.4) | collective-permute-done | bytes 26144 | tf_op jit(solution)/shard_map/ppermute | solution.py:15
  51.2 1.9 %collective-permute-start.5 = (bf16[2,51,256]{2,1,0:T(8,128)(2,1)S(1)}, bf16[2,51,256]{2,1,0:T(8,128)(2,1)S(1)}, u32[]{:S(2)}, u32[]{:S(2)}) collective-permute-start(bf16[2,51,256]{2,1,0:T(8,128)(2,1)S(1)} %pad_maximum_fusion.5), channel_id=1, source_target_pairs={{0,4},{1,5},{2,6},{3,7},{4,0},{5,1},{6,2},{7,3},{8,12},{9,13},{10,... | collective-permute-start | bytes 156680 | tf_op jit(solution)/shard_map/ppermute | solution.py:15
  53.1 0.0 collective-permute-done.10
  53.1 0.3 pad_maximum_fusion.1
  53.4 0.1 collective-permute-start.11
  53.5 2.0 %collective-permute-done.5 = bf16[2,51,256]{2,1,0:T(8,128)(2,1)S(1)} collective-permute-done((bf16[2,51,256]{2,1,0:T(8,128)(2,1)S(1)}, bf16[2,51,256]{2,1,0:T(8,128)(2,1)S(1)}, u32[]{:S(2)}, u32[]{:S(2)}) %collective-permute-start.5) | collective-permute-done | bytes 52256 | tf_op jit(solution)/shard_map/ppermute | solution.py:15
  55.5 2.4 %collective-permute-start.6 = (bf16[4,51,256]{2,1,0:T(8,128)(2,1)S(1)}, bf16[4,51,256]{2,1,0:T(8,128)(2,1)S(1)}, u32[]{:S(2)}, u32[]{:S(2)}) collective-permute-start(bf16[4,51,256]{2,1,0:T(8,128)(2,1)S(1)} %pad_maximum_fusion.2), channel_id=1, source_target_pairs={{0,8},{1,9},{2,10},{3,11},{4,12},{5,13},{6,14},{7,15},{8,0},{9,1},... | collective-permute-start | bytes 313352 | tf_op jit(solution)/shard_map/ppermute | solution.py:15
  57.9 3.4 %collective-permute-done.6 = bf16[4,51,256]{2,1,0:T(8,128)(2,1)S(1)} collective-permute-done((bf16[4,51,256]{2,1,0:T(8,128)(2,1)S(1)}, bf16[4,51,256]{2,1,0:T(8,128)(2,1)S(1)}, u32[]{:S(2)}, u32[]{:S(2)}) %collective-permute-start.6) | collective-permute-done | bytes 104480 | tf_op jit(solution)/shard_map/ppermute | solution.py:15
  61.3 0.1 collective-permute-start.7
  61.4 0.0 collective-permute-done.11
  61.4 1.3 %concatenate.65 = bf16[16,14336]{1,0:T(8,128)(2,1)S(1)} concatenate(bf16[1,14336]{1,0:T(2,128)(2,1)S(1)} %copy-done.1, bf16[1,14336]{1,0:T(2,128)(2,1)S(1)} %collective-permute-done.8, bf16[2,14336]{1,0:T(2,128)(2,1)S(1)} %collective-permute-done.9, bf16[4,14336]{1,0:T(4,128)(2,1)S(1)} %collective-permute-done.10, bf16[8,14336]{1,0:T(8,128)(2,1)} %collective-permute-done.11), dimensions={0} | concatenate | bytes 917504 | tf_op jit(solution)/shard_map/concatenate | solution.py:27
  62.7 11.8 %fusion.6 = f32[16,896]{1,0:T(8,128)S(1)} fusion(bf16[16,14336]{1,0:T(8,128)(2,1)S(1)} %concatenate.65, bf16[896,14336]{1,0:T(8,128)(2,1)} %param.13), kind=kOutput, calls=%fused_computation.14 | convolution fusion | flops 411070464 | bytes 26206208 | tf_op jit(solution)/shard_map/dot_general | solution.py:39
  74.6 0.0 collective-permute-done.7
  74.6 1.0 constant_dynamic-update-slice_fusion
  75.6 0.6 gather_fusion.2
  76.1 0.1 broadcast_select_fusion
  76.3 0.6 convert_reduce_fusion
  77.6 0.6 gather_fusion.3
  78.3 0.1 broadcast_select_fusion.1
  78.4 9.8 %multiply_reduce_fusion = f32[16,32]{1,0:T(8,128)S(1)} fusion(f32[32,896]{1,0:T(8,128)S(1)} %copy-done.4, f32[16,896]{1,0:T(8,128)S(1)} %fusion.6, f32[896,4096]{1,0:T(8,128)} %param.14, f32[]{:T(128)S(6)} %div.10, bf16[32,4096]{1,0:T(8,128)(2,1)S(1)} %bitcast.35, bf16[16,4096]{1,0:T(8,128)(2,1)S(1)} %broadcast_select_fusion.1), kind=kOutput, calls=%fused_computation.10 | convolution fusion | flops 3772579328 | bytes 15247364 | tf_op jit(solution)/shard_map/dot_general | solution.py:39
  88.2 0.6 collective-permute-start.12
  88.7 0.8 collective-permute-done.12
  89.6 2.4 %collective-permute-start.13 = (f32[4,32]{1,0:T(4,128)S(1)}, f32[4,32]{1,0:T(4,128)S(1)}, u32[]{:S(2)}, u32[]{:S(2)}) collective-permute-start(f32[4,32]{1,0:T(4,128)S(1)} %slice.45), channel_id=1, source_target_pairs={{0,8},{1,9},{2,10},{3,11},{4,12},{5,13},{6,14},{7,15},{8,0},{9,1},... | collective-permute-start | bytes 1544 | tf_op jit(solution)/shard_map/ppermute | solution.py:15
  92.0 2.1 %collective-permute-done.13 = f32[4,32]{1,0:T(4,128)S(1)} collective-permute-done((f32[4,32]{1,0:T(4,128)S(1)}, f32[4,32]{1,0:T(4,128)S(1)}, u32[]{:S(2)}, u32[]{:S(2)}) %collective-permute-start.13) | collective-permute-done | bytes 544 | tf_op jit(solution)/shard_map/ppermute | solution.py:15
  94.1 2.1 %collective-permute-start.14 = (f32[2,32]{1,0:T(2,128)S(1)}, f32[2,32]{1,0:T(2,128)S(1)}, u32[]{:S(2)}, u32[]{:S(2)}) collective-permute-start(f32[2,32]{1,0:T(2,128)S(1)} %slice.47), channel_id=1, source_target_pairs={{0,4},{1,5},{2,6},{3,7},{4,0},{5,1},{6,2},{7,3},{8,12},{9,13},{10,... | collective-permute-start | bytes 776 | tf_op jit(solution)/shard_map/ppermute | solution.py:15
  96.1 1.5 %collective-permute-done.14 = f32[2,32]{1,0:T(2,128)S(1)} collective-permute-done((f32[2,32]{1,0:T(2,128)S(1)}, f32[2,32]{1,0:T(2,128)S(1)}, u32[]{:S(2)}, u32[]{:S(2)}) %collective-permute-start.14) | collective-permute-done | bytes 288 | tf_op jit(solution)/shard_map/ppermute | solution.py:15
  97.7 1.5 %collective-permute-start.15 = (f32[1,32]{1,0:T(1,128)S(1)}, f32[1,32]{1,0:T(1,128)S(1)}, u32[]{:S(2)}, u32[]{:S(2)}) collective-permute-start(f32[1,32]{1,0:T(1,128)S(1)} %slice.49), channel_id=1, source_target_pairs={{0,2},{1,3},{2,0},{3,1},{4,6},{5,7},{6,4},{7,5},{8,10},{9,11},{10,... | collective-permute-start | bytes 392 | tf_op jit(solution)/shard_map/ppermute | solution.py:15
  99.2 2.0 %collective-permute-done.15 = f32[1,32]{1,0:T(1,128)S(1)} collective-permute-done((f32[1,32]{1,0:T(1,128)S(1)}, f32[1,32]{1,0:T(1,128)S(1)}, u32[]{:S(2)}, u32[]{:S(2)}) %collective-permute-start.15) | collective-permute-done | bytes 160 | tf_op jit(solution)/shard_map/ppermute | solution.py:15
  101.2 0.5 slice_add_fusion.3
  (29 shorter events, 0.3 us)
Async XLA Ops:
  0.0 18.2 %copy-start = (bf16[256,4096]{1,0:T(8,128)(2,1)S(1)}, bf16[256,4096]{1,0:T(8,128)(2,1)}, u32[]{:S(2)}) copy-start(bf16[256,4096]{1,0:T(8,128)(2,1)} %param.12) | copy-start | bytes 6291460
  0.0 40.5 %collective-permute-start.8 = (bf16[1,14336]{1,0:T(2,128)(2,1)}, bf16[1,14336]{1,0:T(2,128)(2,1)S(1)}, u32[]{:S(2)}, u32[]{:S(2)}) collective-permute-start(bf16[1,14336]{1,0:T(2,128)(2,1)} %param.9), channel_id=1, source_target_pairs={{0,2},{1,3},{2,0},{3,1},{4,6},{5,7},{6,4},{7,5},{8,10},{9,11},{10,... | collective-permute-start | bytes 86024 | tf_op jit(solution)/shard_map/ppermute | solution.py:15
  3.0 30.5 %collective-permute-start = (bf16[1,4096]{1,0:T(2,128)(2,1)}, bf16[1,4096]{1,0:T(2,128)(2,1)S(1)}, u32[]{:S(2)}, u32[]{:S(2)}) collective-permute-start(bf16[1,4096]{1,0:T(2,128)(2,1)} %param.8), channel_id=1, source_target_pairs={{0,2},{1,3},{2,0},{3,1},{4,6},{5,7},{6,4},{7,5},{8,10},{9,11},{10,... | collective-permute-start | bytes 24584 | tf_op jit(solution)/shard_map/ppermute | solution.py:15
  5.1 13.2 %copy-start.2 = (bf16[32,4096]{1,0:T(8,128)(2,1)S(1)}, bf16[32,4096]{1,0:T(8,128)(2,1)}, u32[]{:S(2)}) copy-start(bf16[32,4096]{1,0:T(8,128)(2,1)} %param.10) | copy-start | bytes 786436
  19.0 14.5 %copy-start.3 = (bf16[1,4096]{1,0:T(2,128)(2,1)S(1)}, bf16[1,4096]{1,0:T(2,128)(2,1)}, u32[]{:S(2)}) copy-start(bf16[1,4096]{1,0:T(2,128)(2,1)} %param.8) | copy-start | bytes 24580
  19.0 21.5 %copy-start.1 = (bf16[1,14336]{1,0:T(2,128)(2,1)S(1)}, bf16[1,14336]{1,0:T(2,128)(2,1)}, u32[]{:S(2)}) copy-start(bf16[1,14336]{1,0:T(2,128)(2,1)} %param.9) | copy-start | bytes 86020
  33.6 3.8 %collective-permute-start.1 = (bf16[2,4096]{1,0:T(2,128)(2,1)S(1)}, bf16[2,4096]{1,0:T(2,128)(2,1)S(1)}, u32[]{:S(2)}, u32[]{:S(2)}) collective-permute-start(bf16[2,4096]{1,0:T(2,128)(2,1)S(1)} %pad_maximum_fusion.8), channel_id=1, source_target_pairs={{0,4},{1,5},{2,6},{3,7},{4,0},{5,1},{6,2},{7,3},{8,12},{9,13},{10,... | collective-permute-start | bytes 49160 | tf_op jit(solution)/shard_map/ppermute | solution.py:15
  37.5 5.0 %collective-permute-start.2 = (bf16[4,4096]{1,0:T(4,128)(2,1)S(1)}, bf16[4,4096]{1,0:T(4,128)(2,1)S(1)}, u32[]{:S(2)}, u32[]{:S(2)}) collective-permute-start(bf16[4,4096]{1,0:T(4,128)(2,1)S(1)} %pad_maximum_fusion.7), channel_id=1, source_target_pairs={{0,8},{1,9},{2,10},{3,11},{4,12},{5,13},{6,14},{7,15},{8,0},{9,1},... | collective-permute-start | bytes 98312 | tf_op jit(solution)/shard_map/ppermute | solution.py:15
  40.7 4.2 %collective-permute-start.9 = (bf16[2,14336]{1,0:T(2,128)(2,1)S(1)}, bf16[2,14336]{1,0:T(2,128)(2,1)S(1)}, u32[]{:S(2)}, u32[]{:S(2)}) collective-permute-start(bf16[2,14336]{1,0:T(2,128)(2,1)S(1)} %pad_maximum_fusion.6), channel_id=1, source_target_pairs={{0,4},{1,5},{2,6},{3,7},{4,0},{5,1},{6,2},{7,3},{8,12},{9,13},{10,... | collective-permute-start | bytes 172040 | tf_op jit(solution)/shard_map/ppermute | solution.py:15
  42.5 3.3 %collective-permute-start.3 = (bf16[8,4096]{1,0:T(8,128)(2,1)S(1)}, bf16[8,4096]{1,0:T(8,128)(2,1)S(1)}, u32[]{:S(2)}, u32[]{:S(2)}) collective-permute-start(bf16[8,4096]{1,0:T(8,128)(2,1)S(1)} %pad_maximum_fusion.4), channel_id=1, source_target_pairs={{0,1},{1,0},{2,3},{3,2},{4,5},{5,4},{6,7},{7,6},{8,9},{9,8},{10,11... | collective-permute-start | bytes 196616 | tf_op jit(solution)/shard_map/ppermute | solution.py:15
  45.1 8.0 %collective-permute-start.10 = (bf16[4,14336]{1,0:T(4,128)(2,1)S(1)}, bf16[4,14336]{1,0:T(4,128)(2,1)S(1)}, u32[]{:S(2)}, u32[]{:S(2)}) collective-permute-start(bf16[4,14336]{1,0:T(4,128)(2,1)S(1)} %pad_maximum_fusion.3), channel_id=1, source_target_pairs={{0,8},{1,9},{2,10},{3,11},{4,12},{5,13},{6,14},{7,15},{8,0},{9,1},... | collective-permute-start | bytes 344072 | tf_op jit(solution)/shard_map/ppermute | solution.py:15
  47.3 3.9 %collective-permute-start.4 = (bf16[1,51,256]{2,1,0:T(8,128)(2,1)S(1)}, bf16[1,51,256]{2,1,0:T(8,128)(2,1)S(1)}, u32[]{:S(2)}, u32[]{:S(2)}) collective-permute-start(bf16[1,51,256]{2,1,0:T(8,128)(2,1)S(1)} %maximum_bitcast_fusion), channel_id=1, source_target_pairs={{0,2},{1,3},{2,0},{3,1},{4,6},{5,7},{6,4},{7,5},{8,10},{9,11},{10,... | collective-permute-start | bytes 78344 | tf_op jit(solution)/shard_map/ppermute | solution.py:15
  51.2 4.2 %collective-permute-start.5 = (bf16[2,51,256]{2,1,0:T(8,128)(2,1)S(1)}, bf16[2,51,256]{2,1,0:T(8,128)(2,1)S(1)}, u32[]{:S(2)}, u32[]{:S(2)}) collective-permute-start(bf16[2,51,256]{2,1,0:T(8,128)(2,1)S(1)} %pad_maximum_fusion.5), channel_id=1, source_target_pairs={{0,4},{1,5},{2,6},{3,7},{4,0},{5,1},{6,2},{7,3},{8,12},{9,13},{10,... | collective-permute-start | bytes 156680 | tf_op jit(solution)/shard_map/ppermute | solution.py:15
  53.4 8.0 %collective-permute-start.11 = (bf16[8,14336]{1,0:T(8,128)(2,1)S(1)}, bf16[8,14336]{1,0:T(8,128)(2,1)}, u32[]{:S(2)}, u32[]{:S(2)}) collective-permute-start(bf16[8,14336]{1,0:T(8,128)(2,1)S(1)} %pad_maximum_fusion.1), channel_id=1, source_target_pairs={{0,1},{1,0},{2,3},{3,2},{4,5},{5,4},{6,7},{7,6},{8,9},{9,8},{10,11... | collective-permute-start | bytes 688136 | tf_op jit(solution)/shard_map/ppermute | solution.py:15
  55.5 5.8 %collective-permute-start.6 = (bf16[4,51,256]{2,1,0:T(8,128)(2,1)S(1)}, bf16[4,51,256]{2,1,0:T(8,128)(2,1)S(1)}, u32[]{:S(2)}, u32[]{:S(2)}) collective-permute-start(bf16[4,51,256]{2,1,0:T(8,128)(2,1)S(1)} %pad_maximum_fusion.2), channel_id=1, source_target_pairs={{0,8},{1,9},{2,10},{3,11},{4,12},{5,13},{6,14},{7,15},{8,0},{9,1},... | collective-permute-start | bytes 313352 | tf_op jit(solution)/shard_map/ppermute | solution.py:15
  61.3 13.3 %collective-permute-start.7 = (bf16[8,51,256]{2,1,0:T(8,128)(2,1)S(1)}, bf16[8,51,256]{2,1,0:T(8,128)(2,1)}, u32[]{:S(2)}, u32[]{:S(2)}) collective-permute-start(bf16[8,51,256]{2,1,0:T(8,128)(2,1)S(1)} %pad_maximum_fusion), channel_id=1, source_target_pairs={{0,1},{1,0},{2,3},{3,2},{4,5},{5,4},{6,7},{7,6},{8,9},{9,8},{10,11... | collective-permute-start | bytes 626696 | tf_op jit(solution)/shard_map/ppermute | solution.py:15
  62.7 15.6 %copy-start.4 = (f32[32,896]{1,0:T(8,128)S(1)}, f32[32,896]{1,0:T(8,128)}, u32[]{:S(2)}) copy-start(f32[32,896]{1,0:T(8,128)} %fusion.5) | copy-start | bytes 344068
  88.2 1.4 %collective-permute-start.12 = (f32[8,32]{1,0:T(8,128)S(1)}, f32[8,32]{1,0:T(8,128)S(1)}, u32[]{:S(2)}, u32[]{:S(2)}) collective-permute-start(f32[8,32]{1,0:T(8,128)S(1)} %slice.63), channel_id=1, source_target_pairs={{0,1},{1,0},{2,3},{3,2},{4,5},{5,4},{6,7},{7,6},{8,9},{9,8},{10,11... | collective-permute-start | bytes 3080 | tf_op jit(solution)/shard_map/ppermute | solution.py:15
  89.6 4.5 %collective-permute-start.13 = (f32[4,32]{1,0:T(4,128)S(1)}, f32[4,32]{1,0:T(4,128)S(1)}, u32[]{:S(2)}, u32[]{:S(2)}) collective-permute-start(f32[4,32]{1,0:T(4,128)S(1)} %slice.45), channel_id=1, source_target_pairs={{0,8},{1,9},{2,10},{3,11},{4,12},{5,13},{6,14},{7,15},{8,0},{9,1},... | collective-permute-start | bytes 1544 | tf_op jit(solution)/shard_map/ppermute | solution.py:15
  94.1 3.6 %collective-permute-start.14 = (f32[2,32]{1,0:T(2,128)S(1)}, f32[2,32]{1,0:T(2,128)S(1)}, u32[]{:S(2)}, u32[]{:S(2)}) collective-permute-start(f32[2,32]{1,0:T(2,128)S(1)} %slice.47), channel_id=1, source_target_pairs={{0,4},{1,5},{2,6},{3,7},{4,0},{5,1},{6,2},{7,3},{8,12},{9,13},{10,... | collective-permute-start | bytes 776 | tf_op jit(solution)/shard_map/ppermute | solution.py:15
  97.7 3.5 %collective-permute-start.15 = (f32[1,32]{1,0:T(1,128)S(1)}, f32[1,32]{1,0:T(1,128)S(1)}, u32[]{:S(2)}, u32[]{:S(2)}) collective-permute-start(f32[1,32]{1,0:T(1,128)S(1)} %slice.49), channel_id=1, source_target_pairs={{0,2},{1,3},{2,0},{3,1},{4,6},{5,7},{6,4},{7,5},{8,10},{9,11},{10,... | collective-permute-start | bytes 392 | tf_op jit(solution)/shard_map/ppermute | solution.py:15

commit v2 on v1

v2 whole, which is shorter than its diff:
```python
import jax
import jax.numpy as jnp
from jax import lax
from jax.experimental import pallas as pl
from jax.experimental.pallas import tpu as pltpu
from jax.sharding import PartitionSpec as P

CONTRACT = (((1,), (1,)), ((), ()))
SUM_ROWS = 8
BF16, F32 = jnp.bfloat16, jnp.float32
VMEM, SMEM = pltpu.VMEM, pltpu.SMEM


def stage_bits(count):
    return [1 << k for k in range(count.bit_length() - 1)][::-1]


def swap(piece, bit, count):
    return lax.ppermute(piece, "blk", [(i, i ^ bit) for i in range(count)])


def slot_order(count):
    order = [0]
    for bit in stage_bits(count):
        order = order + [j ^ bit for j in order]
    return order


def gather_slots(piece, count):
    for bit in stage_bits(count):
        piece = jnp.concatenate([piece, swap(piece, bit, count)], axis=0)
    return piece


def scatter_slots(piece, count):
    for bit in reversed(stage_bits(count)):
        half = piece.shape[0] // 2
        piece = piece[:half] + swap(piece[half:], bit, count)
    return piece


def dot(left, right):
    return lax.dot_general(left, right, CONTRACT, preferred_element_type=F32)


def slot_of(position, count):
    bits = count.bit_length() - 1
    out = jnp.zeros_like(position)
    for k in range(bits):
        out = out | (((position >> k) & 1) << (bits - 1 - k))
    return out


def row_permutation(me, count, local, transposed):
    n = count * local
    a = lax.broadcasted_iota(jnp.int32, (n, n), 0)
    b = lax.broadcasted_iota(jnp.int32, (n, n), 1)
    device, slot = (b, a) if transposed else (a, b)
    same = (device // local == (slot_of(slot // local, count) ^ me)) & (device % local == slot % local)
    return same.astype(F32).astype(BF16)


def whole(space=VMEM):
    return pl.BlockSpec(memory_space=space)


def sum_kernel(after_ref, before_ref, eig_ref, out_ref):
    @pl.when(pl.program_id(0) == 0)
    def _():
        out_ref[...] = before_ref[...]

    rows, columns = eig_ref.shape
    acc = eig_ref[:8, :]
    for i in range(1, rows // 8):
        acc = acc + eig_ref[i * 8 : (i + 1) * 8, :]
    part = acc[:, :128]
    for i in range(1, columns // 128):
        part = part + acc[:, i * 128 : (i + 1) * 128]
    out_ref[...] += part


def query_kernel(after_ref, query_ref, basis_ref, out_ref):
    out_ref[...] = dot(query_ref[...], basis_ref[...]).astype(BF16)


def train_kernel(count, local, d_in, me_ref, near_ref, far_ref, basis_ref, query_ref, sum_ref, out_ref):
    n_train = count * local
    queries = query_ref.shape[0]
    rows = jnp.concatenate([near_ref[:, :d_in], far_ref[:, :d_in]], axis=0)
    rotated = dot(rows, basis_ref[...]).astype(BF16)
    order = row_permutation(me_ref[0], count, local, False)
    out_ref[:n_train, :] = jnp.dot(order, rotated, preferred_element_type=F32).astype(BF16)
    out_ref[n_train : n_train + queries, :] = query_ref[...]
    whole_sum = jnp.full((SUM_ROWS, out_ref.shape[1]), jnp.sum(sum_ref[...]), F32)
    high = whole_sum.astype(BF16).astype(F32)
    middle = (whole_sum - high).astype(BF16).astype(F32)
    low = whole_sum - high - middle
    row = lax.broadcasted_iota(jnp.int32, whole_sum.shape, 0)
    pieces = jnp.where(row == 0, high, jnp.where(row == 1, middle, jnp.where(row == 2, low, 0.0)))
    out_ref[n_train + queries :, :] = pieces.astype(BF16)


def stack_kernel(d_in, near_ref, far_ref, query_ref, out_ref):
    half = near_ref.shape[0]
    out_ref[: 2 * half, :] = jnp.concatenate([near_ref[:, d_in:], far_ref[:, d_in:]], axis=0)
    out_ref[2 * half :, :] = query_ref[...]


def out_kernel(after_ref, before_ref, stacked_ref, basis_ref, out_ref):
    @pl.when(pl.program_id(0) == 0)
    def _():
        out_ref[...] = before_ref[...]

    out_ref[...] += dot(basis_ref[...], stacked_ref[...])


def first_out_kernel(after_ref, stacked_ref, basis_ref, out_ref):
    part = dot(basis_ref[...], stacked_ref[...])

    @pl.when(pl.program_id(0) == 0)
    def _():
        out_ref[...] = part

    @pl.when(pl.program_id(0) > 0)
    def _():
        out_ref[...] += part


def pack_kernel(d_in, in_ref, out_ref, held_ref):
    held_ref[:, :d_in] = in_ref[...]
    held_ref[:, d_in:] = out_ref[...]


def join_kernel(after_ref, near_ref, far_ref, out_ref):
    half = near_ref.shape[0]
    out_ref[:half] = near_ref[...]
    out_ref[half:] = far_ref[...]


def main_kernel(count, local, queries, scale, chunks, deep, *refs):
    me_ref, sums_near, sums_far, near_ref, far_ref, eig_ref, out_ref, terms_ref, acc, eig, sems = refs
    me = me_ref[0]
    n_train = count * local
    half, _, width = near_ref.shape
    copies = []
    for j, slot in enumerate(chunks):
        column = j * width if slot is None else pl.multiple_of((me ^ slot) * width, width)
        copies.append(pltpu.make_async_copy(eig_ref.at[:, pl.ds(column, width)], eig.at[j], sems.at[j]))
    for copy in copies[:deep]:
        copy.start()
    first = n_train + queries
    total = jnp.sum(sums_near[:, first:, :].astype(F32)) + jnp.sum(sums_far[:, first:, :].astype(F32))
    damping = total / sums_near.shape[2] * scale
    order = row_permutation(me, count, local, True)

    def operands(j):
        copies[j].wait()
        if j + deep < len(chunks):
            copies[j + deep].start()
        inverse = (1.0 / (eig[j] + damping)).astype(BF16)
        block = near_ref.at[j] if j < half else far_ref.at[j - half]
        rows = jnp.dot(order, block[:n_train, :], preferred_element_type=F32).astype(BF16)
        pair = rows[:, None, :] * block[n_train:first, :][None, :, :]
        return inverse, pair.reshape(n_train * queries, width)

    ready = operands(0)
    for j in range(len(chunks)):
        inverse, pair = ready
        if j + 1 < len(chunks):
            ready = operands(j + 1)
        part = dot(inverse, pair)
        if j == 0:
            acc[...] = part
        else:
            acc[...] += part
    pairs = n_train * queries
    column = lax.broadcasted_iota(jnp.int32, (n_train, pairs), 1)
    row = lax.broadcasted_iota(jnp.int32, (n_train, pairs), 0)
    spread_train = (column // queries == row).astype(F32).astype(BF16)
    column = lax.broadcasted_iota(jnp.int32, (queries, pairs), 1)
    row = lax.broadcasted_iota(jnp.int32, (queries, pairs), 0)
    spread_query = (column % queries == row).astype(F32).astype(BF16)
    out = out_ref[...].astype(BF16)
    weight = jnp.dot(out[:, :n_train], spread_train, preferred_element_type=F32)
    weight = weight * jnp.dot(out[:, n_train:], spread_query, preferred_element_type=F32)
    terms_ref[...] = jnp.sum(acc[...] * weight, axis=0, keepdims=True)


def make_shards(count, d_in, d_out):
    def shards(train_in, train_out, query_in, query_out, basis_in, basis_out, eigvals):
        me = lax.axis_index("blk").astype(jnp.int32).reshape(1)
        local = train_in.shape[0]
        queries = query_in.shape[0]
        width = basis_in.shape[0]
        rows = basis_out.shape[0]
        n_train = local * count
        bits = stage_bits(count)
        pieces = 4 if rows % 64 == 0 else 1
        piece = rows // pieces
        steps = 2 if piece % 32 == 0 else 1
        block = piece // steps
        params = pltpu.CompilerParams(vmem_limit_bytes=32 * 2**20)
        eig_far = pltpu.with_memory_space_constraint(eigvals, pltpu.HBM)
        basis_far = pltpu.with_memory_space_constraint(basis_out, pltpu.HBM)

        def eig_sum(index, after, before):
            return pl.pallas_call(
                sum_kernel,
                grid=(steps,),
                out_shape=jax.ShapeDtypeStruct((8, 128), F32),
                in_specs=[
                    whole(pl.ANY),
                    pl.BlockSpec((8, 128), lambda i: (0, 0)),
                    pl.BlockSpec((block, d_in), lambda i: (index * steps + i, 0)),
                ],
                out_specs=pl.BlockSpec((8, 128), lambda i: (0, 0)),
                compiler_params=params,
                cost_estimate=pl.CostEstimate(flops=piece * d_in, bytes_accessed=4 * piece * d_in, transcendentals=0),
                name="eig_sum",
            )(after, before, eig_far)

        stretch = 896 if d_out % (len(bits) * 896) == 0 else d_out // len(bits)
        stretches = d_out // len(bits) // stretch if len(bits) == 4 else d_out // stretch

        def rotate_out(index, after, before, stacked):
            shape = (rows, n_train + queries)
            out = pl.BlockSpec(shape, lambda i: (0, 0))
            places = [
                pl.BlockSpec((shape[1], stretch), lambda i: (0, index * stretches + i)),
                pl.BlockSpec((rows, stretch), lambda i: (0, index * stretches + i)),
            ]
            return pl.pallas_call(
                first_out_kernel if before is None else out_kernel,
                grid=(stretches,),
                out_shape=jax.ShapeDtypeStruct(shape, F32),
                in_specs=[whole(pl.ANY)] + ([] if before is None else [out]) + places,
                out_specs=out,
                compiler_params=params,
                cost_estimate=pl.CostEstimate(
                    flops=2 * rows * stretch * stretches * shape[1],
                    bytes_accessed=2 * rows * stretch * stretches,
                    transcendentals=0,
                ),
                name="rotate_out",
            )(after, *([] if before is None else [before]), stacked, basis_far)

        def join(after, near, far):
            return pl.pallas_call(
                join_kernel,
                out_shape=jax.ShapeDtypeStruct((2 * near.shape[0],) + near.shape[1:], near.dtype),
                in_specs=[whole(pl.ANY), whole(), whole()],
                out_specs=whole(),
                compiler_params=params,
                name="join",
            )(after, near, far)

        held = pl.pallas_call(
            lambda in_ref, out_ref, held_ref: pack_kernel(d_in, in_ref, out_ref, held_ref),
            out_shape=jax.ShapeDtypeStruct((local, d_in + d_out), BF16),
            in_specs=[whole()] * 2,
            out_specs=whole(),
            compiler_params=params,
            name="pack",
        )(train_in, train_out)
        total = jnp.zeros((8, 128), F32)
        query_part = None
        after = me
        for k, bit in enumerate(bits):
            got = swap(held, bit, count)
            if k == min(1, len(bits) - 1):
                query_part = pl.pallas_call(
                    query_kernel,
                    out_shape=jax.ShapeDtypeStruct((queries, width), BF16),
                    in_specs=[whole(pl.ANY), whole(), whole()],
                    out_specs=whole(),
                    compiler_params=params,
                    name="query_in",
                )(after, query_in, basis_in)
            if k < pieces:
                total = eig_sum(k, after, total)
            after = got
            if k < len(bits) - 1:
                held = join(total, held, got)
        near, far = held, got
        parts = pl.pallas_call(
            lambda *refs: train_kernel(count, local, d_in, *refs),
            out_shape=jax.ShapeDtypeStruct((n_train + queries + SUM_ROWS, width), BF16),
            in_specs=[whole(SMEM)] + [whole()] * 5,
            out_specs=whole(),
            compiler_params=params,
            name="train_in",
        )(me, near, far, basis_in, query_part, total)
        stacked = pl.pallas_call(
            lambda *refs: stack_kernel(d_in, *refs),
            out_shape=jax.ShapeDtypeStruct((n_train + queries, d_out), BF16),
            in_specs=[whole()] * 3,
            out_specs=whole(),
            compiler_params=params,
            name="stack",
        )(near, far, query_out)
        held = parts[None]
        after = parts
        out_part = None
        for k, bit in enumerate(bits):
            got = swap(held, bit, count)
            if (k + 1) * stretch * stretches <= d_out:
                out_part = rotate_out(k, after, out_part, stacked)
            after = got
            if k < len(bits) - 1:
                held = join(out_part, held, got)
        near, far = held, got
        sums = (near, far)
        order = slot_order(count)
        if width % 128 == 0:
            chunks = order
        else:
            chunk = 256
            chunks = [None] * (d_in // chunk)
            back = jnp.argsort(jnp.asarray(order, jnp.int32))[me[0] ^ jnp.arange(count)]
            flat = jnp.take(jnp.concatenate([near, far], axis=0), back, axis=0).transpose(1, 0, 2)
            flat = flat.reshape(flat.shape[0], len(chunks), chunk).transpose(1, 0, 2)
            near, far = flat[: len(chunks) // 2], flat[len(chunks) // 2 :]
        terms = pl.pallas_call(
            lambda *refs: main_kernel(count, local, queries, 0.1 / (d_out * d_in), chunks, 4, *refs),
            out_shape=jax.ShapeDtypeStruct((1, n_train * queries), F32),
            in_specs=[whole(SMEM)] + [whole()] * 4 + [whole(pltpu.HBM), whole()],
            out_specs=whole(),
            scratch_shapes=[
                pltpu.VMEM((rows, n_train * queries), F32),
                pltpu.VMEM((len(chunks), rows, near.shape[2]), F32),
                pltpu.SemaphoreType.DMA((len(chunks),)),
            ],
            compiler_params=params,
            name="scores",
        )(me, *sums, near, far, eig_far, out_part)
        return scatter_slots(terms.reshape(n_train, queries), count)

    return shards


def solution(mesh):
    in_specs = (
        P(("groups", "blk"), None),
        P(("groups", "blk"), None),
        P("groups", None),
        P("groups", None),
        P(("groups", "blk"), None),
        P(("groups", "blk"), None),
        P(("groups", "blk"), None),
    )
    out_specs = P(("groups", "blk"), None)
    count = mesh.shape["blk"]

    def run(train_in, train_out, query_in, query_out, basis_in, basis_out, eigvals):
        shards = make_shards(count, train_in.shape[1], train_out.shape[1])
        return jax.shard_map(shards, mesh=mesh, in_specs=in_specs, out_specs=out_specs, check_vma=False)(
            train_in, train_out, query_in, query_out, basis_in, basis_out, eigvals
        )

    return run
```

time: 102 us -> 70.2 us (0.69)
  Pallas kernels: 0 us -> 37.5 us
  matrix products: 36.2 us -> 0 us
  other arithmetic: 12.7 us -> 0.52 us
  starting transfers between devices: 23.1 us -> 13.5 us
  between operations: 5.83 us -> 0.23 us
  local copies, waits for them, and re-layouts: 5.68 us -> 1.75 us
  waiting for transfers between devices: 18.2 us -> 16.4 us
    pallas_call x0 -> x19, Pallas kernels: none -> 37.5 us  [the longest x4 19.1 us: rotate_out(): pl.pallas_call(first_out_kernel if before is None else out_kernel, grid=(...]
    dot_general x5 -> x0, matrix products: 36.2 us -> none  [dot(): lax.dot_general(left, right, CONTRACT, preferred_element_type=jnp.float32)]
    reduce_sum x2 -> x0, other arithmetic: 10.2 us -> none  [the longest x1 9.57 us: shards(): sums = jnp.broadcast_to(split_sum(jnp.sum(eigvals))[:, None], (3, width))]
    ppermute x16 -> x12, starting transfers between devices: 23.1 us -> 13.5 us  [swap(): return lax.ppermute(piece, 'blk', [(i, i ^ bit) for i in range(count)])]
    gather x4 -> x0, local copies, waits for them, and re-layouts: 3.13 us -> none  [the longest x1 1.32 us: shards(): jnp.argsort(order)[me ^ jnp.arange(count)]]
    concatenate x3 -> x0, local copies, waits for them, and re-layouts: 2.4 us -> none  [gather_slots(): piece = jnp.concatenate([piece, swap(piece, bit, count)], axis=0)]
    ppermute x16 -> x12, waiting for transfers between devices: 18.2 us -> 16.4 us  [swap(): return lax.ppermute(piece, 'blk', [(i, i ^ bit) for i in range(count)])]
    unnamed x15 -> x10, local copies, waits for them, and re-layouts: 0.07 us -> 1.55 us
  transfers between devices with their start and end apart: 16 -> 12, of which waited for: 10 -> 7; matrix products, arithmetic and copies ran while one was open for 40% -> 0% of each run, Pallas kernels for 0% -> 41%
where the time goes in v2:
time: 70.2 us; the launch traced here: 69.9 us
  Pallas kernels  37.5 us (53%)
  waiting for transfers between devices  16.4 us (23%)
  starting transfers between devices  13.5 us (19%)
  local copies, waits for them, and re-layouts  1.75 us (2%)
    pallas_call x4, Pallas kernels, rotate_out(): pl.pallas_call(first_out_kernel if before is None else out_kernel, grid=(...  19.1 us
    ppermute x12, waiting for transfers between devices, swap(): return lax.ppermute(piece, 'blk', [(i, i ^ bit) for i in range(count)])  16.4 us
    ppermute x12, starting transfers between devices, swap(): return lax.ppermute(piece, 'blk', [(i, i ^ bit) for i in range(count)])  13.5 us
    pallas_call x4, Pallas kernels, eig_sum(): pl.pallas_call(sum_kernel, grid=(steps,), out_shape=jax.ShapeDtypeStruct(...  8.65 us
    pallas_call x1, Pallas kernels, shards(): pl.pallas_call(lambda *refs: main_kernel(count, local, queries, 0.1 / (d_...  8.02 us
    unnamed x10, local copies, waits for them, and re-layouts  1.55 us
  transfers between devices with their start and end apart: 12, of which 7 were waited for; matrix products, arithmetic and copies ran while one was open for 0% of the time, Pallas kernels for 41%

profile of v2, /device:TPU:0, one launch (start us, length us, event | category | flops | bytes accessed | tf_op | source)
XLA Modules:
  0.0 69.9 jit_solution(7983608546846424656)
XLA Ops:
  0.0 0.0 copy-start.3
  0.0 0.8 %copy-done.3 = bf16[1,14336]{1,0:T(2,128)(2,1)S(1)} copy-done((bf16[1,14336]{1,0:T(2,128)(2,1)S(1)}, bf16[1,14336]{1,0:T(2,128)(2,1)}, u32[]{:S(2)}) %copy-start.3) | copy-done | bytes 28696
  0.8 0.0 copy-start.4
  0.8 0.7 %copy-done.4 = bf16[1,4096]{1,0:T(2,128)(2,1)S(1)} copy-done((bf16[1,4096]{1,0:T(2,128)(2,1)S(1)}, bf16[1,4096]{1,0:T(2,128)(2,1)}, u32[]{:S(2)}) %copy-start.4) | copy-done | bytes 8216
  1.6 4.1 %collective-permute-start = (bf16[1,18432]{1,0:T(2,128)(2,1)S(1)}, bf16[1,18432]{1,0:T(2,128)(2,1)S(1)}, u32[]{:S(2)}, u32[]{:S(2)}) collective-permute-start(bf16[1,18432]{1,0:T(2,128)(2,1)S(1)} %pack.1.near_ref), channel_id=1, source_target_pairs={{0,8},{1,9},{2,10},{3,11},{4,12},{5,13},{6,14},{7,15},{8,0},{9,1},... | collective-permute-start | bytes 110600 | tf_op jit(solution)/shard_map/ppermute | solution.py:19
  5.7 2.2 %eig_sum.4.after_ref.before_ref = f32[8,128]{1,0:T(8,128)S(1)} custom-call(s32[1]{0:T(128)} %bitcast.after_ref.refs_0_, f32[8,128]{1,0:T(8,128)S(1)} %broadcast_in_dim.6.before_ref, f32[896,4096]{1,0:T(8,128)} %refs_5_.1), custom_call_target="tpu_custom_call" | custom-call | flops 917504 | bytes 3670016 | tf_op jit(solution)/shard_map/eig_sum/pallas_call | solution.py:207
  7.8 1.7 %collective-permute-done.far_ref.after_ref = bf16[1,18432]{1,0:T(2,128)(2,1)S(1)} collective-permute-done((bf16[1,18432]{1,0:T(2,128)(2,1)S(1)}, bf16[1,18432]{1,0:T(2,128)(2,1)S(1)}, u32[]{:S(2)}, u32[]{:S(2)}) %collective-permute-start) | collective-permute-done | bytes 36896 | tf_op jit(solution)/shard_map/ppermute | solution.py:19
  9.6 0.0 copy-start
  9.6 0.0 copy-start.2
  9.6 0.7 %collective-permute-start.1 = (bf16[2,18432]{1,0:T(2,128)(2,1)S(1)}, bf16[2,18432]{1,0:T(2,128)(2,1)S(1)}, u32[]{:S(2)}, u32[]{:S(2)}) collective-permute-start(bf16[2,18432]{1,0:T(2,128)(2,1)S(1)} %join.6.near_ref), channel_id=1, source_target_pairs={{0,4},{1,5},{2,6},{3,7},{4,0},{5,1},{6,2},{7,3},{8,12},{9,13},{10,... | collective-permute-start | bytes 221192 | tf_op jit(solution)/shard_map/ppermute | solution.py:19
  10.3 2.2 %eig_sum.5.before_ref.after_ref = f32[8,128]{1,0:T(8,128)S(1)} custom-call(bf16[1,18432]{1,0:T(2,128)(2,1)S(1)} %collective-permute-done.far_ref.after_ref, f32[8,128]{1,0:T(8,128)S(1)} %eig_sum.4.after_ref.before_ref, f32[896,4096]{1,0:T(8,128)} %refs_5_.1), custom_call_target="tpu_custom_call" | custom-call | flops 917504 | bytes 3670016 | tf_op jit(solution)/shard_map/eig_sum/pallas_call | solution.py:207
  12.5 1.5 %collective-permute-done.1.after_ref.far_ref = bf16[2,18432]{1,0:T(2,128)(2,1)S(1)} collective-permute-done((bf16[2,18432]{1,0:T(2,128)(2,1)S(1)}, bf16[2,18432]{1,0:T(2,128)(2,1)S(1)}, u32[]{:S(2)}, u32[]{:S(2)}) %collective-permute-start.1) | collective-permute-done | bytes 73760 | tf_op jit(solution)/shard_map/ppermute | solution.py:19
  14.1 0.0 copy-start.1
  14.1 1.8 %collective-permute-start.2 = (bf16[4,18432]{1,0:T(4,128)(2,1)S(1)}, bf16[4,18432]{1,0:T(4,128)(2,1)S(1)}, u32[]{:S(2)}, u32[]{:S(2)}) collective-permute-start(bf16[4,18432]{1,0:T(4,128)(2,1)S(1)} %join.7.near_ref), channel_id=1, source_target_pairs={{0,2},{1,3},{2,0},{3,1},{4,6},{5,7},{6,4},{7,5},{8,10},{9,11},{10,... | collective-permute-start | bytes 442376 | tf_op jit(solution)/shard_map/ppermute | solution.py:19
  15.9 2.2 %eig_sum.6.after_ref.before_ref = f32[8,128]{1,0:T(8,128)S(1)} custom-call(bf16[2,18432]{1,0:T(2,128)(2,1)S(1)} %collective-permute-done.1.after_ref.far_ref, f32[8,128]{1,0:T(8,128)S(1)} %eig_sum.5.before_ref.after_ref, f32[896,4096]{1,0:T(8,128)} %refs_5_.1), custom_call_target="tpu_custom_call" | custom-call | flops 917504 | bytes 3670016 | tf_op jit(solution)/shard_map/eig_sum/pallas_call | solution.py:207
  18.1 1.3 %collective-permute-done.2.far_ref.after_ref = bf16[4,18432]{1,0:T(4,128)(2,1)S(1)} collective-permute-done((bf16[4,18432]{1,0:T(4,128)(2,1)S(1)}, bf16[4,18432]{1,0:T(4,128)(2,1)S(1)}, u32[]{:S(2)}, u32[]{:S(2)}) %collective-permute-start.2) | collective-permute-done | bytes 147488 | tf_op jit(solution)/shard_map/ppermute | solution.py:19
  19.3 0.1 join.8.refs_1_.refs_0_
  19.4 0.1 collective-permute-start.3
  19.5 0.0 copy-done
  19.5 0.0 copy-done.2
  19.5 0.7 %query_in.1.refs_4_ = bf16[32,256]{1,0:T(8,128)(2,1)S(1)} custom-call(bf16[1,18432]{1,0:T(2,128)(2,1)S(1)} %collective-permute-done.far_ref.after_ref, bf16[32,4096]{1,0:T(8,128)(2,1)S(1)} %copy-done.2, bf16[256,4096]{1,0:T(8,128)(2,1)S(1)} %copy-done), custom_call_target="tpu_custom_call" | custom-call | tf_op jit(solution)/shard_map/query_in/pallas_call | solution.py:271
  20.2 2.2 %eig_sum.7.refs_5_ = f32[8,128]{1,0:T(8,128)S(1)} custom-call(bf16[4,18432]{1,0:T(4,128)(2,1)S(1)} %collective-permute-done.2.far_ref.after_ref, f32[8,128]{1,0:T(8,128)S(1)} %eig_sum.6.after_ref.before_ref, f32[896,4096]{1,0:T(8,128)} %refs_5_.1), custom_call_target="tpu_custom_call" | custom-call | flops 917504 | bytes 3670016 | tf_op jit(solution)/shard_map/eig_sum/pallas_call | solution.py:207
  22.4 0.0 collective-permute-done.3.refs_2_.refs_1_
  22.4 0.8 %train_in.1.after_ref = bf16[56,256]{1,0:T(8,128)(2,1)S(1)} custom-call(s32[1]{0:T(128)} %bitcast.after_ref.refs_0_, bf16[8,18432]{1,0:T(8,128)(2,1)S(1)} %join.8.refs_1_.refs_0_, bf16[8,18432]{1,0:T(8,128)(2,1)S(1)} %collective-permute-done.3.refs_2_.refs_1_, bf16[256,4096]{1,0:T(8,128)(2,1)S(1)} %copy-done, bf16[32,256]{1,0:T(8,128)(2,1)S(1)} %query_in.1.refs_4_, ...), custom_call_target="tpu_custom_call" | custom-call | tf_op jit(solution)/shard_map/train_in/pallas_call | solution.py:285
  23.2 2.0 %collective-permute-start.4 = (bf16[1,56,256]{2,1,0:T(8,128)(2,1)S(1)}, bf16[1,56,256]{2,1,0:T(8,128)(2,1)S(1)}, u32[]{:S(2)}, u32[]{:S(2)}) collective-permute-start(bf16[1,56,256]{2,1,0:T(8,128)(2,1)S(1)} %bitcast.2), channel_id=1, source_target_pairs={{0,8},{1,9},{2,10},{3,11},{4,12},{5,13},{6,14},{7,15},{8,0},{9,1},... | collective-permute-start | bytes 86024 | tf_op jit(solution)/shard_map/ppermute | solution.py:19
  25.2 0.0 copy-done.1
  25.2 0.1 stack.1.stacked_ref
  25.3 4.8 %rotate_out.4.after_ref.before_ref = f32[896,48]{1,0:T(8,128)S(1)} custom-call(bf16[56,256]{1,0:T(8,128)(2,1)S(1)} %train_in.1.after_ref, bf16[48,14336]{1,0:T(8,128)(2,1)S(1)} %stack.1.stacked_ref, bf16[896,14336]{1,0:T(8,128)(2,1)} %basis_ref.9), custom_call_target="tpu_custom_call" | custom-call | flops 308281344 | bytes 6422528 | tf_op jit(solution)/shard_map/rotate_out/pallas_call | solution.py:232
  30.1 0.0 collective-permute-done.4.far_ref.after_ref
  30.2 2.1 %collective-permute-start.5 = (bf16[2,56,256]{2,1,0:T(8,128)(2,1)S(1)}, bf16[2,56,256]{2,1,0:T(8,128)(2,1)S(1)}, u32[]{:S(2)}, u32[]{:S(2)}) collective-permute-start(bf16[2,56,256]{2,1,0:T(8,128)(2,1)S(1)} %join.9.near_ref), channel_id=1, source_target_pairs={{0,4},{1,5},{2,6},{3,7},{4,0},{5,1},{6,2},{7,3},{8,12},{9,13},{10,... | collective-permute-start | bytes 172040 | tf_op jit(solution)/shard_map/ppermute | solution.py:19
  32.3 4.8 %rotate_out.5.before_ref.after_ref = f32[896,48]{1,0:T(8,128)S(1)} custom-call(bf16[1,56,256]{2,1,0:T(8,128)(2,1)S(1)} %collective-permute-done.4.far_ref.after_ref, f32[896,48]{1,0:T(8,128)S(1)} %rotate_out.4.after_ref.before_ref, bf16[48,14336]{1,0:T(8,128)(2,1)S(1)} %stack.1.stacked_ref, bf16[896,14336]{1,0:T(8,128)(2,1)} %basis_ref.9), custom_call_target="tpu_custom_call" | custom-call | flops 308281344 | bytes 6422528 | tf_op jit(solution)/shard_map/rotate_out/pallas_call | solution.py:232
  37.0 0.0 collective-permute-done.5.after_ref.far_ref
  37.1 1.6 %collective-permute-start.6 = (bf16[4,56,256]{2,1,0:T(8,128)(2,1)S(1)}, bf16[4,56,256]{2,1,0:T(8,128)(2,1)S(1)}, u32[]{:S(2)}, u32[]{:S(2)}) collective-permute-start(bf16[4,56,256]{2,1,0:T(8,128)(2,1)S(1)} %join.10.near_ref), channel_id=1, source_target_pairs={{0,2},{1,3},{2,0},{3,1},{4,6},{5,7},{6,4},{7,5},{8,10},{9,11},{10,... | collective-permute-start | bytes 344072 | tf_op jit(solution)/shard_map/ppermute | solution.py:19
  38.7 4.7 %rotate_out.6.after_ref.before_ref = f32[896,48]{1,0:T(8,128)S(1)} custom-call(bf16[2,56,256]{2,1,0:T(8,128)(2,1)S(1)} %collective-permute-done.5.after_ref.far_ref, f32[896,48]{1,0:T(8,128)S(1)} %rotate_out.5.before_ref.after_ref, bf16[48,14336]{1,0:T(8,128)(2,1)S(1)} %stack.1.stacked_ref, bf16[896,14336]{1,0:T(8,128)(2,1)} %basis_ref.9), custom_call_target="tpu_custom_call" | custom-call | flops 308281344 | bytes 6422528 | tf_op jit(solution)/shard_map/rotate_out/pallas_call | solution.py:232
  43.4 0.0 collective-permute-done.6.far_ref.after_ref
  43.4 0.1 collective-permute-start.7
  43.5 4.8 %rotate_out.7.refs_6_ = f32[896,48]{1,0:T(8,128)S(1)} custom-call(bf16[4,56,256]{2,1,0:T(8,128)(2,1)S(1)} %collective-permute-done.6.far_ref.after_ref, f32[896,48]{1,0:T(8,128)S(1)} %rotate_out.6.after_ref.before_ref, bf16[48,14336]{1,0:T(8,128)(2,1)S(1)} %stack.1.stacked_ref, bf16[896,14336]{1,0:T(8,128)(2,1)} %basis_ref.9), custom_call_target="tpu_custom_call" | custom-call | flops 308281344 | bytes 6422528 | tf_op jit(solution)/shard_map/rotate_out/pallas_call | solution.py:232
  48.3 0.0 collective-permute-done.7.refs_2_.refs_4_
  48.3 8.0 %scores.1 = f32[1,512]{1,0:T(1,128)S(1)} custom-call(s32[1]{0:T(128)} %bitcast.after_ref.refs_0_, bf16[8,56,256]{2,1,0:T(8,128)(2,1)S(1)} %join.11.refs_1_.refs_3_, bf16[8,56,256]{2,1,0:T(8,128)(2,1)S(1)} %collective-permute-done.7.refs_2_.refs_4_, bf16[8,56,256]{2,1,0:T(8,128)(2,1)S(1)} %join.11.refs_1_.refs_3_, ...), custom_call_target="tpu_custom_call" | custom-call | tf_op jit(solution)/shard_map/scores/pallas_call | solution.py:323
  56.3 0.1 slice.33
  56.4 0.5 collective-permute-start.8
  56.9 0.1 slice.31
  57.0 0.7 %collective-permute-done.8 = f32[8,32]{1,0:T(8,128)S(1)} collective-permute-done((f32[8,32]{1,0:T(8,128)S(1)}, f32[8,32]{1,0:T(8,128)S(1)}, u32[]{:S(2)}, u32[]{:S(2)}) %collective-permute-start.8) | collective-permute-done | bytes 1056 | tf_op jit(solution)/shard_map/ppermute | solution.py:19
  57.7 0.5 collective-permute-start.9
  58.2 3.1 %collective-permute-done.9 = f32[4,32]{1,0:T(4,128)S(1)} collective-permute-done((f32[4,32]{1,0:T(4,128)S(1)}, f32[4,32]{1,0:T(4,128)S(1)}, u32[]{:S(2)}, u32[]{:S(2)}) %collective-permute-start.9) | collective-permute-done | bytes 544 | tf_op jit(solution)/shard_map/ppermute | solution.py:19
  61.3 0.0 collective-permute-start.10
  61.4 3.5 %collective-permute-done.10 = f32[2,32]{1,0:T(2,128)S(1)} collective-permute-done((f32[2,32]{1,0:T(2,128)S(1)}, f32[2,32]{1,0:T(2,128)S(1)}, u32[]{:S(2)}, u32[]{:S(2)}) %collective-permute-start.10) | collective-permute-done | bytes 288 | tf_op jit(solution)/shard_map/ppermute | solution.py:19
  64.9 0.0 collective-permute-start.11
  64.9 4.4 %collective-permute-done.11 = f32[1,32]{1,0:T(1,128)S(1)} collective-permute-done((f32[1,32]{1,0:T(1,128)S(1)}, f32[1,32]{1,0:T(1,128)S(1)}, u32[]{:S(2)}, u32[]{:S(2)}) %collective-permute-start.11) | collective-permute-done | bytes 160 | tf_op jit(solution)/shard_map/ppermute | solution.py:19
  69.4 0.5 slice_add_fusion.2
  (14 shorter events, 0.2 us)
Async XLA Ops:
  0.0 0.8 %copy-start.3 = (bf16[1,14336]{1,0:T(2,128)(2,1)S(1)}, bf16[1,14336]{1,0:T(2,128)(2,1)}, u32[]{:S(2)}) copy-start(bf16[1,14336]{1,0:T(2,128)(2,1)} %out_ref.1) | copy-start | bytes 86020
  0.8 0.7 %copy-start.4 = (bf16[1,4096]{1,0:T(2,128)(2,1)S(1)}, bf16[1,4096]{1,0:T(2,128)(2,1)}, u32[]{:S(2)}) copy-start(bf16[1,4096]{1,0:T(2,128)(2,1)} %in_ref.1) | copy-start | bytes 24580
  1.6 8.0 %collective-permute-start = (bf16[1,18432]{1,0:T(2,128)(2,1)S(1)}, bf16[1,18432]{1,0:T(2,128)(2,1)S(1)}, u32[]{:S(2)}, u32[]{:S(2)}) collective-permute-start(bf16[1,18432]{1,0:T(2,128)(2,1)S(1)} %pack.1.near_ref), channel_id=1, source_target_pairs={{0,8},{1,9},{2,10},{3,11},{4,12},{5,13},{6,14},{7,15},{8,0},{9,1},... | collective-permute-start | bytes 110600 | tf_op jit(solution)/shard_map/ppermute | solution.py:19
  9.6 9.9 %copy-start = (bf16[256,4096]{1,0:T(8,128)(2,1)S(1)}, bf16[256,4096]{1,0:T(8,128)(2,1)}, u32[]{:S(2)}) copy-start(bf16[256,4096]{1,0:T(8,128)(2,1)} %refs_3_.1) | copy-start | bytes 6291460
  9.6 9.9 %copy-start.2 = (bf16[32,4096]{1,0:T(8,128)(2,1)S(1)}, bf16[32,4096]{1,0:T(8,128)(2,1)}, u32[]{:S(2)}) copy-start(bf16[32,4096]{1,0:T(8,128)(2,1)} %query_ref.1) | copy-start | bytes 786436
  9.6 4.4 %collective-permute-start.1 = (bf16[2,18432]{1,0:T(2,128)(2,1)S(1)}, bf16[2,18432]{1,0:T(2,128)(2,1)S(1)}, u32[]{:S(2)}, u32[]{:S(2)}) collective-permute-start(bf16[2,18432]{1,0:T(2,128)(2,1)S(1)} %join.6.near_ref), channel_id=1, source_target_pairs={{0,4},{1,5},{2,6},{3,7},{4,0},{5,1},{6,2},{7,3},{8,12},{9,13},{10,... | collective-permute-start | bytes 221192 | tf_op jit(solution)/shard_map/ppermute | solution.py:19
  14.1 11.1 %copy-start.1 = (bf16[32,14336]{1,0:T(8,128)(2,1)S(1)}, bf16[32,14336]{1,0:T(8,128)(2,1)}, u32[]{:S(2)}) copy-start(bf16[32,14336]{1,0:T(8,128)(2,1)} %refs_2_.1) | copy-start | bytes 2752516
  14.1 5.2 %collective-permute-start.2 = (bf16[4,18432]{1,0:T(4,128)(2,1)S(1)}, bf16[4,18432]{1,0:T(4,128)(2,1)S(1)}, u32[]{:S(2)}, u32[]{:S(2)}) collective-permute-start(bf16[4,18432]{1,0:T(4,128)(2,1)S(1)} %join.7.near_ref), channel_id=1, source_target_pairs={{0,2},{1,3},{2,0},{3,1},{4,6},{5,7},{6,4},{7,5},{8,10},{9,11},{10,... | collective-permute-start | bytes 442376 | tf_op jit(solution)/shard_map/ppermute | solution.py:19
  19.4 3.0 %collective-permute-start.3 = (bf16[8,18432]{1,0:T(8,128)(2,1)S(1)}, bf16[8,18432]{1,0:T(8,128)(2,1)S(1)}, u32[]{:S(2)}, u32[]{:S(2)}) collective-permute-start(bf16[8,18432]{1,0:T(8,128)(2,1)S(1)} %join.8.refs_1_.refs_0_), channel_id=1, source_target_pairs={{0,1},{1,0},{2,3},{3,2},{4,5},{5,4},{6,7},{7,6},{8,9},{9,8},{10,11... | collective-permute-start | bytes 884744 | tf_op jit(solution)/shard_map/ppermute | solution.py:19
  23.2 7.0 %collective-permute-start.4 = (bf16[1,56,256]{2,1,0:T(8,128)(2,1)S(1)}, bf16[1,56,256]{2,1,0:T(8,128)(2,1)S(1)}, u32[]{:S(2)}, u32[]{:S(2)}) collective-permute-start(bf16[1,56,256]{2,1,0:T(8,128)(2,1)S(1)} %bitcast.2), channel_id=1, source_target_pairs={{0,8},{1,9},{2,10},{3,11},{4,12},{5,13},{6,14},{7,15},{8,0},{9,1},... | collective-permute-start | bytes 86024 | tf_op jit(solution)/shard_map/ppermute | solution.py:19
  30.2 6.9 %collective-permute-start.5 = (bf16[2,56,256]{2,1,0:T(8,128)(2,1)S(1)}, bf16[2,56,256]{2,1,0:T(8,128)(2,1)S(1)}, u32[]{:S(2)}, u32[]{:S(2)}) collective-permute-start(bf16[2,56,256]{2,1,0:T(8,128)(2,1)S(1)} %join.9.near_ref), channel_id=1, source_target_pairs={{0,4},{1,5},{2,6},{3,7},{4,0},{5,1},{6,2},{7,3},{8,12},{9,13},{10,... | collective-permute-start | bytes 172040 | tf_op jit(solution)/shard_map/ppermute | solution.py:19
  37.1 6.3 %collective-permute-start.6 = (bf16[4,56,256]{2,1,0:T(8,128)(2,1)S(1)}, bf16[4,56,256]{2,1,0:T(8,128)(2,1)S(1)}, u32[]{:S(2)}, u32[]{:S(2)}) collective-permute-start(bf16[4,56,256]{2,1,0:T(8,128)(2,1)S(1)} %join.10.near_ref), channel_id=1, source_target_pairs={{0,2},{1,3},{2,0},{3,1},{4,6},{5,7},{6,4},{7,5},{8,10},{9,11},{10,... | collective-permute-start | bytes 344072 | tf_op jit(solution)/shard_map/ppermute | solution.py:19
  43.4 4.8 %collective-permute-start.7 = (bf16[8,56,256]{2,1,0:T(8,128)(2,1)S(1)}, bf16[8,56,256]{2,1,0:T(8,128)(2,1)S(1)}, u32[]{:S(2)}, u32[]{:S(2)}) collective-permute-start(bf16[8,56,256]{2,1,0:T(8,128)(2,1)S(1)} %join.11.refs_1_.refs_3_), channel_id=1, source_target_pairs={{0,1},{1,0},{2,3},{3,2},{4,5},{5,4},{6,7},{7,6},{8,9},{9,8},{10,11... | collective-permute-start | bytes 688136 | tf_op jit(solution)/shard_map/ppermute | solution.py:19
  56.4 1.3 %collective-permute-start.8 = (f32[8,32]{1,0:T(8,128)S(1)}, f32[8,32]{1,0:T(8,128)S(1)}, u32[]{:S(2)}, u32[]{:S(2)}) collective-permute-start(f32[8,32]{1,0:T(8,128)S(1)} %slice.33), channel_id=1, source_target_pairs={{0,1},{1,0},{2,3},{3,2},{4,5},{5,4},{6,7},{7,6},{8,9},{9,8},{10,11... | collective-permute-start | bytes 3080 | tf_op jit(solution)/shard_map/ppermute | solution.py:19
  57.7 3.6 %collective-permute-start.9 = (f32[4,32]{1,0:T(4,128)S(1)}, f32[4,32]{1,0:T(4,128)S(1)}, u32[]{:S(2)}, u32[]{:S(2)}) collective-permute-start(f32[4,32]{1,0:T(4,128)S(1)} %slice.35), channel_id=1, source_target_pairs={{0,2},{1,3},{2,0},{3,1},{4,6},{5,7},{6,4},{7,5},{8,10},{9,11},{10,... | collective-permute-start | bytes 1544 | tf_op jit(solution)/shard_map/ppermute | solution.py:19
  61.3 3.6 %collective-permute-start.10 = (f32[2,32]{1,0:T(2,128)S(1)}, f32[2,32]{1,0:T(2,128)S(1)}, u32[]{:S(2)}, u32[]{:S(2)}) collective-permute-start(f32[2,32]{1,0:T(2,128)S(1)} %slice.37), channel_id=1, source_target_pairs={{0,4},{1,5},{2,6},{3,7},{4,0},{5,1},{6,2},{7,3},{8,12},{9,13},{10,... | collective-permute-start | bytes 776 | tf_op jit(solution)/shard_map/ppermute | solution.py:19
  64.9 4.4 %collective-permute-start.11 = (f32[1,32]{1,0:T(1,128)S(1)}, f32[1,32]{1,0:T(1,128)S(1)}, u32[]{:S(2)}, u32[]{:S(2)}) collective-permute-start(f32[1,32]{1,0:T(1,128)S(1)} %slice.39), channel_id=1, source_target_pairs={{0,8},{1,9},{2,10},{3,11},{4,12},{5,13},{6,14},{7,15},{8,0},{9,1},... | collective-permute-start | bytes 392 | tf_op jit(solution)/shard_map/ppermute | solution.py:19

commit v3 on v2

--- a/solution.py
+++ b/solution.py
@@ -7,6 +7,10 @@
 
 CONTRACT = (((1,), (1,)), ((), ()))
 SUM_ROWS = 8
+class Fixed(int):
+    pass
+
+
 BF16, F32 = jnp.bfloat16, jnp.float32
 VMEM, SMEM = pltpu.VMEM, pltpu.SMEM
 
@@ -106,46 +110,72 @@
     out_ref[2 * half :, :] = query_ref[...]
 
 
-def out_kernel(after_ref, before_ref, stacked_ref, basis_ref, out_ref):
-    @pl.when(pl.program_id(0) == 0)
-    def _():
-        out_ref[...] = before_ref[...]
-
-    out_ref[...] += dot(basis_ref[...], stacked_ref[...])
-
-
-def first_out_kernel(after_ref, stacked_ref, basis_ref, out_ref):
-    part = dot(basis_ref[...], stacked_ref[...])
-
-    @pl.when(pl.program_id(0) == 0)
-    def _():
-        out_ref[...] = part
-
-    @pl.when(pl.program_id(0) > 0)
-    def _():
-        out_ref[...] += part
-
-
-def pack_kernel(d_in, in_ref, out_ref, held_ref):
-    held_ref[:, :d_in] = in_ref[...]
-    held_ref[:, d_in:] = out_ref[...]
-
-
-def join_kernel(after_ref, near_ref, far_ref, out_ref):
+def fetch(basis_ref, begin, width, held_ref, sems):
+    rows = held_ref.shape[0]
+    parts = sems.shape[0]
+    copies = []
+    for c in range(parts):
+        place = pl.ds(c * (rows // parts), rows // parts)
+        copies.append(pltpu.make_async_copy(basis_ref.at[place, pl.ds(begin, width)], held_ref.at[place], sems.at[c]))
+    for copy in copies:
+        copy.start()
+    return copies
+
+
+def load_kernel(begin, after_ref, basis_ref, next_ref, sems):
+    for copy in fetch(basis_ref, begin, next_ref.shape[1], next_ref, sems):
+        copy.wait()
+
+
+def out_kernel(begin, after_ref, before_ref, stacked_ref, held_ref, basis_ref, out_ref, next_ref, sems):
+    width = held_ref.shape[1]
+    copies = fetch(basis_ref, begin + width, next_ref.shape[1], next_ref, sems)
+    out_ref[...] = before_ref[...] + dot(held_ref[...], stacked_ref[:, pl.ds(begin, width)])
+    for copy in copies:
+        copy.wait()
+
+
+def last_out_kernel(begin, chunks, me_ref, after_ref, before_ref, stacked_ref, held_ref, eig_ref, out_ref, early_ref, sems):
+    width = held_ref.shape[1]
+    copies = eig_copies(me_ref[0], chunks, eig_ref, early_ref, sems)
+    for copy in copies:
+        copy.start()
+    out_ref[...] = before_ref[...] + dot(held_ref[...], stacked_ref[:, pl.ds(begin, width)])
+    for copy in copies:
+        copy.wait()
+
+
+def eig_copies(me, chunks, eig_ref, eig, sems):
+    width = eig.shape[2]
+    copies = []
+    for j, slot in enumerate(chunks):
+        column = slot * width if isinstance(slot, Fixed) else pl.multiple_of((me ^ slot) * width, width)
+        copies.append(pltpu.make_async_copy(eig_ref.at[:, pl.ds(column, width)], eig.at[j], sems.at[j]))
+    return copies
+
+
+def pack_kernel(d_in, in_ref, out_ref, held_ref, sems):
+    first = pltpu.make_async_copy(in_ref, held_ref.at[:, :d_in], sems.at[0])
+    second = pltpu.make_async_copy(out_ref, held_ref.at[:, d_in:], sems.at[1])
+    first.start()
+    second.start()
+    first.wait()
+    second.wait()
+
+
+def join_kernel(after_ref, other_ref, near_ref, far_ref, out_ref):
     half = near_ref.shape[0]
     out_ref[:half] = near_ref[...]
     out_ref[half:] = far_ref[...]
 
 
 def main_kernel(count, local, queries, scale, chunks, deep, *refs):
-    me_ref, sums_near, sums_far, near_ref, far_ref, eig_ref, out_ref, terms_ref, acc, eig, sems = refs
+    me_ref, sums_near, sums_far, near_ref, far_ref, eig_ref, early_ref, out_ref, terms_ref, acc, eig, sems = refs
     me = me_ref[0]
     n_train = count * local
     half, _, width = near_ref.shape
-    copies = []
-    for j, slot in enumerate(chunks):
-        column = j * width if slot is None else pl.multiple_of((me ^ slot) * width, width)
-        copies.append(pltpu.make_async_copy(eig_ref.at[:, pl.ds(column, width)], eig.at[j], sems.at[j]))
+    early = early_ref.shape[0]
+    copies = eig_copies(me, chunks[early:], eig_ref, eig, sems)
     for copy in copies[:deep]:
         copy.start()
     first = n_train + queries
@@ -154,10 +184,12 @@
     order = row_permutation(me, count, local, True)
 
     def operands(j):
-        copies[j].wait()
-        if j + deep < len(chunks):
-            copies[j + deep].start()
-        inverse = (1.0 / (eig[j] + damping)).astype(BF16)
+        if j >= early:
+            copies[j - early].wait()
+            if j - early + deep < len(copies):
+                copies[j - early + deep].start()
+        values = early_ref[j] if j < early else eig[j - early]
+        inverse = (1.0 / (values + damping)).astype(BF16)
         block = near_ref.at[j] if j < half else far_ref.at[j - half]
         rows = jnp.dot(order, block[:n_train, :], preferred_element_type=F32).astype(BF16)
         pair = rows[:, None, :] * block[n_train:first, :][None, :, :]
@@ -195,79 +227,107 @@
         rows = basis_out.shape[0]
         n_train = local * count
         bits = stage_bits(count)
-        pieces = 4 if rows % 64 == 0 else 1
-        piece = rows // pieces
-        steps = 2 if piece % 32 == 0 else 1
-        block = piece // steps
-        params = pltpu.CompilerParams(vmem_limit_bytes=32 * 2**20)
+        order = slot_order(count)
+        chunk = width if width % 128 == 0 else 256
+        chunks = order if width % 128 == 0 else [Fixed(k) for k in range(d_in // chunk)]
+        early = min(4, len(chunks) - 1)
+        block = 112 if rows % 112 == 0 else rows
+        blocks = rows // block
+        pieces = max(1, len(bits) - 1)
+        cuts = [-(-k * blocks // pieces) for k in range(pieces + 1)]
+        params = pltpu.CompilerParams(vmem_limit_bytes=20 * 2**20)
         eig_far = pltpu.with_memory_space_constraint(eigvals, pltpu.HBM)
         basis_far = pltpu.with_memory_space_constraint(basis_out, pltpu.HBM)
 
         def eig_sum(index, after, before):
             return pl.pallas_call(
                 sum_kernel,
-                grid=(steps,),
+                grid=(cuts[index + 1] - cuts[index],),
                 out_shape=jax.ShapeDtypeStruct((8, 128), F32),
                 in_specs=[
                     whole(pl.ANY),
                     pl.BlockSpec((8, 128), lambda i: (0, 0)),
-                    pl.BlockSpec((block, d_in), lambda i: (index * steps + i, 0)),
+                    pl.BlockSpec((block, d_in), lambda i: (cuts[index] + i, 0)),
                 ],
                 out_specs=pl.BlockSpec((8, 128), lambda i: (0, 0)),
                 compiler_params=params,
-                cost_estimate=pl.CostEstimate(flops=piece * d_in, bytes_accessed=4 * piece * d_in, transcendentals=0),
+                cost_estimate=pl.CostEstimate(flops=rows * d_in // 4, bytes_accessed=rows * d_in, transcendentals=0),
                 name="eig_sum",
             )(after, before, eig_far)
 
-        stretch = 896 if d_out % (len(bits) * 896) == 0 else d_out // len(bits)
-        stretches = d_out // len(bits) // stretch if len(bits) == 4 else d_out // stretch
-
-        def rotate_out(index, after, before, stacked):
-            shape = (rows, n_train + queries)
-            out = pl.BlockSpec(shape, lambda i: (0, 0))
-            places = [
-                pl.BlockSpec((shape[1], stretch), lambda i: (0, index * stretches + i)),
-                pl.BlockSpec((rows, stretch), lambda i: (0, index * stretches + i)),
-            ]
+        stretch = 128
+        stretches = d_out // stretch
+        turns = min(len(bits), 4)
+        out_cuts = [k * stretches // turns * stretch for k in range(turns + 1)]
+        parts = 4 if rows % 64 == 0 else 1
+
+        def held_shape(index):
+            return jax.ShapeDtypeStruct((rows, out_cuts[index + 1] - out_cuts[index]), BF16)
+
+        def load_first(after):
             return pl.pallas_call(
-                first_out_kernel if before is None else out_kernel,
-                grid=(stretches,),
-                out_shape=jax.ShapeDtypeStruct(shape, F32),
-                in_specs=[whole(pl.ANY)] + ([] if before is None else [out]) + places,
-                out_specs=out,
+                lambda *refs: load_kernel(0, *refs),
+                out_shape=held_shape(0),
+                in_specs=[whole(pl.ANY), whole(pltpu.HBM)],
+                out_specs=whole(),
+                scratch_shapes=[pltpu.SemaphoreType.DMA((parts,))],
                 compiler_params=params,
-                cost_estimate=pl.CostEstimate(
-                    flops=2 * rows * stretch * stretches * shape[1],
-                    bytes_accessed=2 * rows * stretch * stretches,
-                    transcendentals=0,
-                ),
-                name="rotate_out",
-            )(after, *([] if before is None else [before]), stacked, basis_far)
-
-        def join(after, near, far):
+                cost_estimate=pl.CostEstimate(flops=0, bytes_accessed=rows * d_out // 2, transcendentals=0),
+                name="load",
+            )(after, basis_far)
+
+        def rotate_out(index, after, before, stacked, held):
+            out = jax.ShapeDtypeStruct((rows, n_train + queries), F32)
+            cost = pl.CostEstimate(
+                flops=rows * d_out * (n_train + queries) // 2, bytes_accessed=rows * d_out // 2, transcendentals=0
+            )
+            if index + 1 < turns:
+                return pl.pallas_call(
+                    lambda *refs: out_kernel(out_cuts[index], *refs),
+                    out_shape=(out, held_shape(index + 1)),
+                    in_specs=[whole(pl.ANY)] + [whole()] * 3 + [whole(pltpu.HBM)],
+                    out_specs=(whole(), whole()),
+                    scratch_shapes=[pltpu.SemaphoreType.DMA((parts,))],
+                    compiler_params=params,
+                    cost_estimate=cost,
+                    name="rotate_out",
+                )(after, before, stacked, held, basis_far)
+            return pl.pallas_call(
+                lambda *refs: last_out_kernel(out_cuts[index], chunks[:early], *refs),
+                out_shape=(out, jax.ShapeDtypeStruct((early, rows, chunk), F32)),
+                in_specs=[whole(SMEM), whole(pl.ANY)] + [whole()] * 3 + [whole(pltpu.HBM)],
+                out_specs=(whole(), whole()),
+                scratch_shapes=[pltpu.SemaphoreType.DMA((early,))],
+                compiler_params=params,
+                cost_estimate=cost,
+                name="rotate_out_last",
+            )(me, after, before, stacked, held, eig_far)
+
+        def join(after, near, far, other=None):
             return pl.pallas_call(
                 join_kernel,
                 out_shape=jax.ShapeDtypeStruct((2 * near.shape[0],) + near.shape[1:], near.dtype),
-                in_specs=[whole(pl.ANY), whole(), whole()],
+                in_specs=[whole(pl.ANY), whole(pl.ANY), whole(), whole()],
                 out_specs=whole(),
                 compiler_params=params,
                 name="join",
-            )(after, near, far)
+            )(after, after if other is None else other, near, far)
 
         held = pl.pallas_call(
-            lambda in_ref, out_ref, held_ref: pack_kernel(d_in, in_ref, out_ref, held_ref),
+            lambda *refs: pack_kernel(d_in, *refs),
             out_shape=jax.ShapeDtypeStruct((local, d_in + d_out), BF16),
-            in_specs=[whole()] * 2,
+            in_specs=[whole(pltpu.HBM)] * 2,
             out_specs=whole(),
+            scratch_shapes=[pltpu.SemaphoreType.DMA((2,))],
             compiler_params=params,
             name="pack",
-        )(train_in, train_out)
+        )(pltpu.with_memory_space_constraint(train_in, pltpu.HBM), pltpu.with_memory_space_constraint(train_out, pltpu.HBM))
         total = jnp.zeros((8, 128), F32)
         query_part = None
         after = me
         for k, bit in enumerate(bits):
             got = swap(held, bit, count)
-            if k == min(1, len(bits) - 1):
+            if k == min(2, len(bits) - 1):
                 query_part = pl.pallas_call(
                     query_kernel,
                     out_shape=jax.ShapeDtypeStruct((queries, width), BF16),
@@ -276,13 +336,14 @@
                     compiler_params=params,
                     name="query_in",
                 )(after, query_in, basis_in)
-            if k < pieces:
+            if k < pieces and cuts[k] < cuts[k + 1]:
                 total = eig_sum(k, after, total)
             after = got
             if k < len(bits) - 1:
-                held = join(total, held, got)
+                held = join(total, held, got, query_part)
         near, far = held, got
-        parts = pl.pallas_call(
+        basis_held = load_first(held)
+        merged = pl.pallas_call(
             lambda *refs: train_kernel(count, local, d_in, *refs),
             out_shape=jax.ShapeDtypeStruct((n_train + queries + SUM_ROWS, width), BF16),
             in_specs=[whole(SMEM)] + [whole()] * 5,
@@ -298,24 +359,19 @@
             compiler_params=params,
             name="stack",
         )(near, far, query_out)
-        held = parts[None]
-        after = parts
-        out_part = None
+        held = merged[None]
+        after = merged
+        out_part = jnp.zeros((rows, n_train + queries), F32)
         for k, bit in enumerate(bits):
             got = swap(held, bit, count)
-            if (k + 1) * stretch * stretches <= d_out:
-                out_part = rotate_out(k, after, out_part, stacked)
+            if k < turns:
+                out_part, basis_held = rotate_out(k, after, out_part, stacked, basis_held)
             after = got
             if k < len(bits) - 1:
                 held = join(out_part, held, got)
         near, far = held, got
         sums = (near, far)
-        order = slot_order(count)
-        if width % 128 == 0:
-            chunks = order
-        else:
-            chunk = 256
-            chunks = [None] * (d_in // chunk)
+        if isinstance(chunks[0], Fixed):
             back = jnp.argsort(jnp.asarray(order, jnp.int32))[me[0] ^ jnp.arange(count)]
             flat = jnp.take(jnp.concatenate([near, far], axis=0), back, axis=0).transpose(1, 0, 2)
             flat = flat.reshape(flat.shape[0], len(chunks), chunk).transpose(1, 0, 2)
@@ -323,16 +379,16 @@
         terms = pl.pallas_call(
             lambda *refs: main_kernel(count, local, queries, 0.1 / (d_out * d_in), chunks, 4, *refs),
             out_shape=jax.ShapeDtypeStruct((1, n_train * queries), F32),
-            in_specs=[whole(SMEM)] + [whole()] * 4 + [whole(pltpu.HBM), whole()],
+            in_specs=[whole(SMEM)] + [whole()] * 4 + [whole(pltpu.HBM), whole(), whole()],
             out_specs=whole(),
             scratch_shapes=[
                 pltpu.VMEM((rows, n_train * queries), F32),
-                pltpu.VMEM((len(chunks), rows, near.shape[2]), F32),
-                pltpu.SemaphoreType.DMA((len(chunks),)),
+                pltpu.VMEM((len(chunks) - early, rows, chunk), F32),
+                pltpu.SemaphoreType.DMA((len(chunks) - early,)),
             ],
             compiler_params=params,
             name="scores",
-        )(me, *sums, near, far, eig_far, out_part)
+        )(me, *sums, near, far, eig_far, basis_held, out_part)
         return scatter_slots(terms.reshape(n_train, queries), count)
 
     return shards

time: 70.2 us -> 63.7 us (0.907)
  waiting for transfers between devices: 16.4 us -> 9.76 us
  starting transfers between devices: 13.5 us -> 17 us
  Pallas kernels: 37.5 us -> 35.6 us
  local copies, waits for them, and re-layouts: 1.75 us -> 0.25 us
    ppermute x12, waiting for transfers between devices: 16.4 us -> 9.76 us  [swap(): return lax.ppermute(piece, 'blk', [(i, i ^ bit) for i in range(count)])]
    ppermute x12, starting transfers between devices: 13.5 us -> 17 us  [swap(): return lax.ppermute(piece, 'blk', [(i, i ^ bit) for i in range(count)])]
    unnamed x10 -> x6, local copies, waits for them, and re-layouts: 1.55 us -> 0.02 us
    pallas_call x1, Pallas kernels: 8.02 us -> 6.68 us  [shards(): pl.pallas_call(lambda *refs: main_kernel(count, local, queries, 0.1 / (d_...]
  transfers between devices with their start and end apart: 12 -> 12, of which waited for: 7 -> 6; matrix products, arithmetic and copies ran while one was open for 0% -> 0% of each run, Pallas kernels for 41% -> 43%
where the time goes in v3:
time: 63.7 us; the launch traced here: 63.4 us
  Pallas kernels  35.6 us (56%)
  starting transfers between devices  17 us (27%)
  waiting for transfers between devices  9.76 us (15%)
    ppermute x12, starting transfers between devices, swap(): return lax.ppermute(piece, 'blk', [(i, i ^ bit) for i in range(count)])  17 us
    pallas_call x3, Pallas kernels, rotate_out(): pl.pallas_call(lambda *refs: out_kernel(out_cuts[index], *refs), out_shap...  11.1 us
    ppermute x12, waiting for transfers between devices, swap(): return lax.ppermute(piece, 'blk', [(i, i ^ bit) for i in range(count)])  9.76 us
    pallas_call x3, Pallas kernels, eig_sum(): pl.pallas_call(sum_kernel, grid=(cuts[index + 1] - cuts[index],), out_sha...  8.8 us
    pallas_call x1, Pallas kernels, shards(): pl.pallas_call(lambda *refs: main_kernel(count, local, queries, 0.1 / (d_...  6.68 us
    pallas_call x1, Pallas kernels, rotate_out(): pl.pallas_call(lambda *refs: last_out_kernel(out_cuts[index], chunks[:ear...  3.47 us
    pallas_call x1, Pallas kernels, load_first(): pl.pallas_call(lambda *refs: load_kernel(0, *refs), out_shape=held_shape(...  2.97 us
  transfers between devices with their start and end apart: 12, of which 6 were waited for; matrix products, arithmetic and copies ran while one was open for 0% of the time, Pallas kernels for 43%

profile of v3, /device:TPU:0, one launch (start us, length us, event | category | flops | bytes accessed | tf_op | source)
XLA Modules:
  0.0 63.4 jit_solution(10881271088965416729)
XLA Ops:
  0.0 0.9 %pack.1.near_ref = bf16[1,18432]{1,0:T(2,128)(2,1)S(1)} custom-call(bf16[1,4096]{1,0:T(2,128)(2,1)} %refs_0_.1, bf16[1,14336]{1,0:T(2,128)(2,1)} %refs_1_.2), custom_call_target="tpu_custom_call" | custom-call | tf_op jit(solution)/shard_map/pack/pallas_call | solution.py:316
  0.9 4.1 %collective-permute-start = (bf16[1,18432]{1,0:T(2,128)(2,1)S(1)}, bf16[1,18432]{1,0:T(2,128)(2,1)S(1)}, u32[]{:S(2)}, u32[]{:S(2)}) collective-permute-start(bf16[1,18432]{1,0:T(2,128)(2,1)S(1)} %pack.1.near_ref), channel_id=1, source_target_pairs={{0,8},{1,9},{2,10},{3,11},{4,12},{5,13},{6,14},{7,15},{8,0},{9,1},... | collective-permute-start | bytes 110600 | tf_op jit(solution)/shard_map/ppermute | solution.py:23
  5.0 3.3 %eig_sum.3.after_ref.other_ref.before_ref = f32[8,128]{1,0:T(8,128)S(1)} custom-call(s32[1]{0:T(128)} %bitcast.after_ref.refs_0_, f32[8,128]{1,0:T(8,128)S(1)} %broadcast_in_dim.9.before_ref, f32[896,4096]{1,0:T(8,128)} %refs_5_.3), custom_call_target="tpu_custom_call" | custom-call | flops 917504 | bytes 3670016 | tf_op jit(solution)/shard_map/eig_sum/pallas_call | solution.py:243
  8.3 0.6 collective-permute-done.far_ref.after_ref
  8.9 0.0 copy-start
  8.9 0.0 copy-start.2
  8.9 1.1 %collective-permute-start.1 = (bf16[2,18432]{1,0:T(2,128)(2,1)S(1)}, bf16[2,18432]{1,0:T(2,128)(2,1)S(1)}, u32[]{:S(2)}, u32[]{:S(2)}) collective-permute-start(bf16[2,18432]{1,0:T(2,128)(2,1)S(1)} %join.6.near_ref), channel_id=1, source_target_pairs={{0,4},{1,5},{2,6},{3,7},{4,0},{5,1},{6,2},{7,3},{8,12},{9,13},{10,... | collective-permute-start | bytes 221192 | tf_op jit(solution)/shard_map/ppermute | solution.py:23
  10.0 3.3 %eig_sum.4.before_ref.after_ref.other_ref = f32[8,128]{1,0:T(8,128)S(1)} custom-call(bf16[1,18432]{1,0:T(2,128)(2,1)S(1)} %collective-permute-done.far_ref.after_ref, f32[8,128]{1,0:T(8,128)S(1)} %eig_sum.3.after_ref.other_ref.before_ref, f32[896,4096]{1,0:T(8,128)} %refs_5_.3), custom_call_target="tpu_custom_call" | custom-call | flops 917504 | bytes 3670016 | tf_op jit(solution)/shard_map/eig_sum/pallas_call | solution.py:243
  13.3 0.0 collective-permute-done.1.after_ref.far_ref
  13.4 1.8 %collective-permute-start.2 = (bf16[4,18432]{1,0:T(4,128)(2,1)S(1)}, bf16[4,18432]{1,0:T(4,128)(2,1)S(1)}, u32[]{:S(2)}, u32[]{:S(2)}) collective-permute-start(bf16[4,18432]{1,0:T(4,128)(2,1)S(1)} %join.7.near_ref), channel_id=1, source_target_pairs={{0,2},{1,3},{2,0},{3,1},{4,6},{5,7},{6,4},{7,5},{8,10},{9,11},{10,... | collective-permute-start | bytes 442376 | tf_op jit(solution)/shard_map/ppermute | solution.py:23
  15.2 0.0 copy-done
  15.2 0.0 copy-done.2
  15.2 0.7 %query_in.1.other_ref.refs_4_ = bf16[32,256]{1,0:T(8,128)(2,1)S(1)} custom-call(bf16[2,18432]{1,0:T(2,128)(2,1)S(1)} %collective-permute-done.1.after_ref.far_ref, bf16[32,4096]{1,0:T(8,128)(2,1)S(1)} %copy-done.2, bf16[256,4096]{1,0:T(8,128)(2,1)S(1)} %copy-done), custom_call_target="tpu_custom_call" | custom-call | tf_op jit(solution)/shard_map/query_in/pallas_call | solution.py:331
  15.9 2.2 %eig_sum.5.after_ref.refs_5_ = f32[8,128]{1,0:T(8,128)S(1)} custom-call(bf16[2,18432]{1,0:T(2,128)(2,1)S(1)} %collective-permute-done.1.after_ref.far_ref, f32[8,128]{1,0:T(8,128)S(1)} %eig_sum.4.before_ref.after_ref.other_ref, f32[896,4096]{1,0:T(8,128)} %refs_5_.3), custom_call_target="tpu_custom_call" | custom-call | flops 917504 | bytes 3670016 | tf_op jit(solution)/shard_map/eig_sum/pallas_call | solution.py:243
  18.1 0.5 collective-permute-done.2.far_ref
  18.6 0.1 join.8.refs_1_.refs_0_
  18.7 0.0 copy-start.1
  18.7 0.1 collective-permute-start.3
  18.8 3.0 %load.1.refs_3_ = bf16[896,3584]{1,0:T(8,128)(2,1)S(1)} custom-call(bf16[8,18432]{1,0:T(8,128)(2,1)S(1)} %join.8.refs_1_.refs_0_, bf16[896,14336]{1,0:T(8,128)(2,1)} %refs_4_.5), custom_call_target="tpu_custom_call" | custom-call | bytes 6422528 | tf_op jit(solution)/shard_map/load/pallas_call | solution.py:268
  21.7 0.0 collective-permute-done.3.refs_2_.refs_1_
  21.8 0.8 %train_in.1.refs_0_ = bf16[56,256]{1,0:T(8,128)(2,1)S(1)} custom-call(s32[1]{0:T(128)} %bitcast.after_ref.refs_0_, bf16[8,18432]{1,0:T(8,128)(2,1)S(1)} %join.8.refs_1_.refs_0_, bf16[8,18432]{1,0:T(8,128)(2,1)S(1)} %collective-permute-done.3.refs_2_.refs_1_, bf16[256,4096]{1,0:T(8,128)(2,1)S(1)} %copy-done, bf16[32,256]{1,0:T(8,128)(2,1)S(1)} %query_in.1.other_ref.refs_4_, ...), custom_call_target="tpu_custom_call" | custom-call | tf_op jit(solution)/shard_map/train_in/pallas_call | solution.py:346
  22.5 3.1 %collective-permute-start.4 = (bf16[1,56,256]{2,1,0:T(8,128)(2,1)S(1)}, bf16[1,56,256]{2,1,0:T(8,128)(2,1)S(1)}, u32[]{:S(2)}, u32[]{:S(2)}) collective-permute-start(bf16[1,56,256]{2,1,0:T(8,128)(2,1)S(1)} %bitcast.2), channel_id=1, source_target_pairs={{0,8},{1,9},{2,10},{3,11},{4,12},{5,13},{6,14},{7,15},{8,0},{9,1},... | collective-permute-start | bytes 86024 | tf_op jit(solution)/shard_map/ppermute | solution.py:23
  25.7 0.0 copy-done.1
  25.7 0.1 stack.1.refs_2_.refs_3_
  25.8 3.7 %rotate_out.3 = (f32[896,48]{1,0:T(8,128)S(1)}, bf16[896,3584]{1,0:T(8,128)(2,1)S(1)}) custom-call(bf16[56,256]{1,0:T(8,128)(2,1)S(1)} %train_in.1.refs_0_, f32[896,48]{1,0:T(8,128)S(1)} %broadcast_in_dim.10.refs_1_, bf16[48,14336]{1,0:T(8,128)(2,1)S(1)} %stack.1.refs_2_.refs_3_, bf16[896,3584]{1,0:T(8,128)(2,1)S(1)} %load.1.refs_3_, bf16[896,14336]{1,0:T(8,128)(2,1)} %refs_4_.5), custom_call_target="tpu_custom_call" | custom-call | flops 308281344 | bytes 6422528 | tf_op jit(solution)/shard_map/rotate_out/pallas_call | solution.py:285
  29.5 0.0 collective-permute-done.4.far_ref.refs_0_
  29.6 1.0 %collective-permute-start.5 = (bf16[2,56,256]{2,1,0:T(8,128)(2,1)S(1)}, bf16[2,56,256]{2,1,0:T(8,128)(2,1)S(1)}, u32[]{:S(2)}, u32[]{:S(2)}) collective-permute-start(bf16[2,56,256]{2,1,0:T(8,128)(2,1)S(1)} %join.9.near_ref), channel_id=1, source_target_pairs={{0,4},{1,5},{2,6},{3,7},{4,0},{5,1},{6,2},{7,3},{8,12},{9,13},{10,... | collective-permute-start | bytes 172040 | tf_op jit(solution)/shard_map/ppermute | solution.py:23
  30.5 3.7 %rotate_out.4 = (f32[896,48]{1,0:T(8,128)S(1)}, bf16[896,3584]{1,0:T(8,128)(2,1)S(1)}) custom-call(bf16[1,56,256]{2,1,0:T(8,128)(2,1)S(1)} %collective-permute-done.4.far_ref.refs_0_, f32[896,48]{1,0:T(8,128)S(1)} %get-tuple-element.13.after_ref.other_ref.refs_1_, bf16[48,14336]{1,0:T(8,128)(2,1)S(1)} %stack.1.refs_2_.refs_3_, ...), custom_call_target="tpu_custom_call" | custom-call | flops 308281344 | bytes 6422528 | tf_op jit(solution)/shard_map/rotate_out/pallas_call | solution.py:285
  34.2 0.0 collective-permute-done.5.refs_0_.far_ref
  34.3 1.6 %collective-permute-start.6 = (bf16[4,56,256]{2,1,0:T(8,128)(2,1)S(1)}, bf16[4,56,256]{2,1,0:T(8,128)(2,1)S(1)}, u32[]{:S(2)}, u32[]{:S(2)}) collective-permute-start(bf16[4,56,256]{2,1,0:T(8,128)(2,1)S(1)} %join.10.near_ref), channel_id=1, source_target_pairs={{0,2},{1,3},{2,0},{3,1},{4,6},{5,7},{6,4},{7,5},{8,10},{9,11},{10,... | collective-permute-start | bytes 344072 | tf_op jit(solution)/shard_map/ppermute | solution.py:23
  35.9 3.7 %rotate_out.5 = (f32[896,48]{1,0:T(8,128)S(1)}, bf16[896,3584]{1,0:T(8,128)(2,1)S(1)}) custom-call(bf16[2,56,256]{2,1,0:T(8,128)(2,1)S(1)} %collective-permute-done.5.refs_0_.far_ref, f32[896,48]{1,0:T(8,128)S(1)} %get-tuple-element.15.refs_1_.after_ref.other_ref, bf16[48,14336]{1,0:T(8,128)(2,1)S(1)} %stack.1.refs_2_.refs_3_, ...), custom_call_target="tpu_custom_call" | custom-call | flops 308281344 | bytes 6422528 | tf_op jit(solution)/shard_map/rotate_out/pallas_call | solution.py:285
  39.6 0.0 collective-permute-done.6.far_ref.refs_1_
  39.6 0.1 collective-permute-start.7
  39.7 3.5 %rotate_out_last.1 = (f32[896,48]{1,0:T(8,128)S(1)}, f32[4,896,256]{2,1,0:T(8,128)S(1)}) custom-call(s32[1]{0:T(128)} %bitcast.after_ref.refs_0_, bf16[4,56,256]{2,1,0:T(8,128)(2,1)S(1)} %collective-permute-done.6.far_ref.refs_1_, f32[896,48]{1,0:T(8,128)S(1)} %get-tuple-element.17.after_ref.other_ref.refs_2_, bf16[48,14336]{1,0:T(8,128)(2,1)S(1)} %stack.1.refs_2_.refs_3_, ...), custom_call_target="tpu_custom_call" | custom-call | flops 308281344 | bytes 6422528 | tf_op jit(solution)/shard_map/rotate_out_last/pallas_call | solution.py:295
  43.2 0.0 collective-permute-done.7.refs_2_.refs_4_
  43.2 6.7 %scores.1 = f32[1,512]{1,0:T(1,128)S(1)} custom-call(s32[1]{0:T(128)} %bitcast.after_ref.refs_0_, bf16[8,56,256]{2,1,0:T(8,128)(2,1)S(1)} %join.11.refs_1_.refs_3_, bf16[8,56,256]{2,1,0:T(8,128)(2,1)S(1)} %collective-permute-done.7.refs_2_.refs_4_, bf16[8,56,256]{2,1,0:T(8,128)(2,1)S(1)} %join.11.refs_1_.refs_3_, ...), custom_call_target="tpu_custom_call" | custom-call | tf_op jit(solution)/shard_map/scores/pallas_call | solution.py:379
  49.9 0.1 slice.33
  50.0 0.5 collective-permute-start.8
  50.5 0.1 slice.31
  50.5 0.7 %collective-permute-done.8 = f32[8,32]{1,0:T(8,128)S(1)} collective-permute-done((f32[8,32]{1,0:T(8,128)S(1)}, f32[8,32]{1,0:T(8,128)S(1)}, u32[]{:S(2)}, u32[]{:S(2)}) %collective-permute-start.8) | collective-permute-done | bytes 1056 | tf_op jit(solution)/shard_map/ppermute | solution.py:23
  51.3 1.2 %collective-permute-start.9 = (f32[4,32]{1,0:T(4,128)S(1)}, f32[4,32]{1,0:T(4,128)S(1)}, u32[]{:S(2)}, u32[]{:S(2)}) collective-permute-start(f32[4,32]{1,0:T(4,128)S(1)} %slice.35), channel_id=1, source_target_pairs={{0,2},{1,3},{2,0},{3,1},{4,6},{5,7},{6,4},{7,5},{8,10},{9,11},{10,... | collective-permute-start | bytes 1544 | tf_op jit(solution)/shard_map/ppermute | solution.py:23
  52.5 2.4 %collective-permute-done.9 = f32[4,32]{1,0:T(4,128)S(1)} collective-permute-done((f32[4,32]{1,0:T(4,128)S(1)}, f32[4,32]{1,0:T(4,128)S(1)}, u32[]{:S(2)}, u32[]{:S(2)}) %collective-permute-start.9) | collective-permute-done | bytes 544 | tf_op jit(solution)/shard_map/ppermute | solution.py:23
  54.9 1.1 %collective-permute-start.10 = (f32[2,32]{1,0:T(2,128)S(1)}, f32[2,32]{1,0:T(2,128)S(1)}, u32[]{:S(2)}, u32[]{:S(2)}) collective-permute-start(f32[2,32]{1,0:T(2,128)S(1)} %slice.37), channel_id=1, source_target_pairs={{0,4},{1,5},{2,6},{3,7},{4,0},{5,1},{6,2},{7,3},{8,12},{9,13},{10,... | collective-permute-start | bytes 776 | tf_op jit(solution)/shard_map/ppermute | solution.py:23
  56.0 2.5 %collective-permute-done.10 = f32[2,32]{1,0:T(2,128)S(1)} collective-permute-done((f32[2,32]{1,0:T(2,128)S(1)}, f32[2,32]{1,0:T(2,128)S(1)}, u32[]{:S(2)}, u32[]{:S(2)}) %collective-permute-start.10) | collective-permute-done | bytes 288 | tf_op jit(solution)/shard_map/ppermute | solution.py:23
  58.5 1.4 %collective-permute-start.11 = (f32[1,32]{1,0:T(1,128)S(1)}, f32[1,32]{1,0:T(1,128)S(1)}, u32[]{:S(2)}, u32[]{:S(2)}) collective-permute-start(f32[1,32]{1,0:T(1,128)S(1)} %slice.39), channel_id=1, source_target_pairs={{0,8},{1,9},{2,10},{3,11},{4,12},{5,13},{6,14},{7,15},{8,0},{9,1},... | collective-permute-start | bytes 392 | tf_op jit(solution)/shard_map/ppermute | solution.py:23
  59.9 3.0 %collective-permute-done.11 = f32[1,32]{1,0:T(1,128)S(1)} collective-permute-done((f32[1,32]{1,0:T(1,128)S(1)}, f32[1,32]{1,0:T(1,128)S(1)}, u32[]{:S(2)}, u32[]{:S(2)}) %collective-permute-start.11) | collective-permute-done | bytes 160 | tf_op jit(solution)/shard_map/ppermute | solution.py:23
  62.9 0.5 slice_add_fusion.2
  (14 shorter events, 0.2 us)
Async XLA Ops:
  0.9 8.0 %collective-permute-start = (bf16[1,18432]{1,0:T(2,128)(2,1)S(1)}, bf16[1,18432]{1,0:T(2,128)(2,1)S(1)}, u32[]{:S(2)}, u32[]{:S(2)}) collective-permute-start(bf16[1,18432]{1,0:T(2,128)(2,1)S(1)} %pack.1.near_ref), channel_id=1, source_target_pairs={{0,8},{1,9},{2,10},{3,11},{4,12},{5,13},{6,14},{7,15},{8,0},{9,1},... | collective-permute-start | bytes 110600 | tf_op jit(solution)/shard_map/ppermute | solution.py:23
  8.9 6.3 %copy-start = (bf16[256,4096]{1,0:T(8,128)(2,1)S(1)}, bf16[256,4096]{1,0:T(8,128)(2,1)}, u32[]{:S(2)}) copy-start(bf16[256,4096]{1,0:T(8,128)(2,1)} %refs_3_.1) | copy-start | bytes 6291460
  8.9 6.3 %copy-start.2 = (bf16[32,4096]{1,0:T(8,128)(2,1)S(1)}, bf16[32,4096]{1,0:T(8,128)(2,1)}, u32[]{:S(2)}) copy-start(bf16[32,4096]{1,0:T(8,128)(2,1)} %query_ref.1) | copy-start | bytes 786436
  8.9 4.4 %collective-permute-start.1 = (bf16[2,18432]{1,0:T(2,128)(2,1)S(1)}, bf16[2,18432]{1,0:T(2,128)(2,1)S(1)}, u32[]{:S(2)}, u32[]{:S(2)}) collective-permute-start(bf16[2,18432]{1,0:T(2,128)(2,1)S(1)} %join.6.near_ref), channel_id=1, source_target_pairs={{0,4},{1,5},{2,6},{3,7},{4,0},{5,1},{6,2},{7,3},{8,12},{9,13},{10,... | collective-permute-start | bytes 221192 | tf_op jit(solution)/shard_map/ppermute | solution.py:23
  13.4 5.2 %collective-permute-start.2 = (bf16[4,18432]{1,0:T(4,128)(2,1)S(1)}, bf16[4,18432]{1,0:T(4,128)(2,1)S(1)}, u32[]{:S(2)}, u32[]{:S(2)}) collective-permute-start(bf16[4,18432]{1,0:T(4,128)(2,1)S(1)} %join.7.near_ref), channel_id=1, source_target_pairs={{0,2},{1,3},{2,0},{3,1},{4,6},{5,7},{6,4},{7,5},{8,10},{9,11},{10,... | collective-permute-start | bytes 442376 | tf_op jit(solution)/shard_map/ppermute | solution.py:23
  18.7 7.0 %copy-start.1 = (bf16[32,14336]{1,0:T(8,128)(2,1)S(1)}, bf16[32,14336]{1,0:T(8,128)(2,1)}, u32[]{:S(2)}) copy-start(bf16[32,14336]{1,0:T(8,128)(2,1)} %refs_2_.1) | copy-start | bytes 2752516
  18.7 3.1 %collective-permute-start.3 = (bf16[8,18432]{1,0:T(8,128)(2,1)S(1)}, bf16[8,18432]{1,0:T(8,128)(2,1)S(1)}, u32[]{:S(2)}, u32[]{:S(2)}) collective-permute-start(bf16[8,18432]{1,0:T(8,128)(2,1)S(1)} %join.8.refs_1_.refs_0_), channel_id=1, source_target_pairs={{0,1},{1,0},{2,3},{3,2},{4,5},{5,4},{6,7},{7,6},{8,9},{9,8},{10,11... | collective-permute-start | bytes 884744 | tf_op jit(solution)/shard_map/ppermute | solution.py:23
  22.5 7.0 %collective-permute-start.4 = (bf16[1,56,256]{2,1,0:T(8,128)(2,1)S(1)}, bf16[1,56,256]{2,1,0:T(8,128)(2,1)S(1)}, u32[]{:S(2)}, u32[]{:S(2)}) collective-permute-start(bf16[1,56,256]{2,1,0:T(8,128)(2,1)S(1)} %bitcast.2), channel_id=1, source_target_pairs={{0,8},{1,9},{2,10},{3,11},{4,12},{5,13},{6,14},{7,15},{8,0},{9,1},... | collective-permute-start | bytes 86024 | tf_op jit(solution)/shard_map/ppermute | solution.py:23
  29.6 4.7 %collective-permute-start.5 = (bf16[2,56,256]{2,1,0:T(8,128)(2,1)S(1)}, bf16[2,56,256]{2,1,0:T(8,128)(2,1)S(1)}, u32[]{:S(2)}, u32[]{:S(2)}) collective-permute-start(bf16[2,56,256]{2,1,0:T(8,128)(2,1)S(1)} %join.9.near_ref), channel_id=1, source_target_pairs={{0,4},{1,5},{2,6},{3,7},{4,0},{5,1},{6,2},{7,3},{8,12},{9,13},{10,... | collective-permute-start | bytes 172040 | tf_op jit(solution)/shard_map/ppermute | solution.py:23
  34.3 5.3 %collective-permute-start.6 = (bf16[4,56,256]{2,1,0:T(8,128)(2,1)S(1)}, bf16[4,56,256]{2,1,0:T(8,128)(2,1)S(1)}, u32[]{:S(2)}, u32[]{:S(2)}) collective-permute-start(bf16[4,56,256]{2,1,0:T(8,128)(2,1)S(1)} %join.10.near_ref), channel_id=1, source_target_pairs={{0,2},{1,3},{2,0},{3,1},{4,6},{5,7},{6,4},{7,5},{8,10},{9,11},{10,... | collective-permute-start | bytes 344072 | tf_op jit(solution)/shard_map/ppermute | solution.py:23
  39.6 3.6 %collective-permute-start.7 = (bf16[8,56,256]{2,1,0:T(8,128)(2,1)S(1)}, bf16[8,56,256]{2,1,0:T(8,128)(2,1)S(1)}, u32[]{:S(2)}, u32[]{:S(2)}) collective-permute-start(bf16[8,56,256]{2,1,0:T(8,128)(2,1)S(1)} %join.11.refs_1_.refs_3_), channel_id=1, source_target_pairs={{0,1},{1,0},{2,3},{3,2},{4,5},{5,4},{6,7},{7,6},{8,9},{9,8},{10,11... | collective-permute-start | bytes 688136 | tf_op jit(solution)/shard_map/ppermute | solution.py:23
  50.0 1.3 %collective-permute-start.8 = (f32[8,32]{1,0:T(8,128)S(1)}, f32[8,32]{1,0:T(8,128)S(1)}, u32[]{:S(2)}, u32[]{:S(2)}) collective-permute-start(f32[8,32]{1,0:T(8,128)S(1)} %slice.33), channel_id=1, source_target_pairs={{0,1},{1,0},{2,3},{3,2},{4,5},{5,4},{6,7},{7,6},{8,9},{9,8},{10,11... | collective-permute-start | bytes 3080 | tf_op jit(solution)/shard_map/ppermute | solution.py:23
  51.3 3.6 %collective-permute-start.9 = (f32[4,32]{1,0:T(4,128)S(1)}, f32[4,32]{1,0:T(4,128)S(1)}, u32[]{:S(2)}, u32[]{:S(2)}) collective-permute-start(f32[4,32]{1,0:T(4,128)S(1)} %slice.35), channel_id=1, source_target_pairs={{0,2},{1,3},{2,0},{3,1},{4,6},{5,7},{6,4},{7,5},{8,10},{9,11},{10,... | collective-permute-start | bytes 1544 | tf_op jit(solution)/shard_map/ppermute | solution.py:23
  54.9 3.6 %collective-permute-start.10 = (f32[2,32]{1,0:T(2,128)S(1)}, f32[2,32]{1,0:T(2,128)S(1)}, u32[]{:S(2)}, u32[]{:S(2)}) collective-permute-start(f32[2,32]{1,0:T(2,128)S(1)} %slice.37), channel_id=1, source_target_pairs={{0,4},{1,5},{2,6},{3,7},{4,0},{5,1},{6,2},{7,3},{8,12},{9,13},{10,... | collective-permute-start | bytes 776 | tf_op jit(solution)/shard_map/ppermute | solution.py:23
  58.5 4.4 %collective-permute-start.11 = (f32[1,32]{1,0:T(1,128)S(1)}, f32[1,32]{1,0:T(1,128)S(1)}, u32[]{:S(2)}, u32[]{:S(2)}) collective-permute-start(f32[1,32]{1,0:T(1,128)S(1)} %slice.39), channel_id=1, source_target_pairs={{0,8},{1,9},{2,10},{3,11},{4,12},{5,13},{6,14},{7,15},{8,0},{9,1},... | collective-permute-start | bytes 392 | tf_op jit(solution)/shard_map/ppermute | solution.py:23

commit v4 on v3

--- a/solution.py
+++ b/solution.py
@@ -230,7 +230,7 @@
         order = slot_order(count)
         chunk = width if width % 128 == 0 else 256
         chunks = order if width % 128 == 0 else [Fixed(k) for k in range(d_in // chunk)]
-        early = min(4, len(chunks) - 1)
+        early = min(2, len(chunks) - 1)
         block = 112 if rows % 112 == 0 else rows
         blocks = rows // block
         pieces = max(1, len(bits) - 1)
@@ -259,7 +259,7 @@
         stretches = d_out // stretch
         turns = min(len(bits), 4)
         out_cuts = [k * stretches // turns * stretch for k in range(turns + 1)]
-        parts = 4 if rows % 64 == 0 else 1
+        parts = 8 if rows % 128 == 0 else 1
 
         def held_shape(index):
             return jax.ShapeDtypeStruct((rows, out_cuts[index + 1] - out_cuts[index]), BF16)

time: 63.7 us -> 61.4 us (0.964)
  Pallas kernels: 35.6 us -> 33.1 us
  starting transfers between devices: 17 us -> 17.7 us
    pallas_call x3, Pallas kernels: 11.1 us -> 9.4 us  [rotate_out(): pl.pallas_call(lambda *refs: out_kernel(out_cuts[index], *refs), out_shap...]
    pallas_call x1, Pallas kernels: 3.47 us -> 1.85 us  [rotate_out(): pl.pallas_call(lambda *refs: last_out_kernel(out_cuts[index], chunks[:ear...]
    pallas_call x1, Pallas kernels: 6.68 us -> 7.48 us  [shards(): pl.pallas_call(lambda *refs: main_kernel(count, local, queries, 0.1 / (d_...]
    ppermute x12, starting transfers between devices: 17 us -> 17.7 us  [swap(): return lax.ppermute(piece, 'blk', [(i, i ^ bit) for i in range(count)])]
  transfers between devices with their start and end apart: 12 -> 12, of which waited for: 6 -> 8; matrix products, arithmetic and copies ran while one was open for 0% -> 0% of each run, Pallas kernels for 43% -> 39%
where the time goes in v4:
time: 61.4 us; the launch traced here: 61.2 us
  Pallas kernels  33.1 us (54%)
  starting transfers between devices  17.7 us (29%)
  waiting for transfers between devices  9.32 us (15%)
    ppermute x12, starting transfers between devices, swap(): return lax.ppermute(piece, 'blk', [(i, i ^ bit) for i in range(count)])  17.7 us
    pallas_call x3, Pallas kernels, rotate_out(): pl.pallas_call(lambda *refs: out_kernel(out_cuts[index], *refs), out_shap...  9.4 us
    ppermute x12, waiting for transfers between devices, swap(): return lax.ppermute(piece, 'blk', [(i, i ^ bit) for i in range(count)])  9.32 us
    pallas_call x3, Pallas kernels, eig_sum(): pl.pallas_call(sum_kernel, grid=(cuts[index + 1] - cuts[index],), out_sha...  8.8 us
    pallas_call x1, Pallas kernels, shards(): pl.pallas_call(lambda *refs: main_kernel(count, local, queries, 0.1 / (d_...  7.48 us
    pallas_call x1, Pallas kernels, load_first(): pl.pallas_call(lambda *refs: load_kernel(0, *refs), out_shape=held_shape(...  2.96 us
    pallas_call x1, Pallas kernels, rotate_out(): pl.pallas_call(lambda *refs: last_out_kernel(out_cuts[index], chunks[:ear...  1.85 us
  transfers between devices with their start and end apart: 12, of which 8 were waited for; matrix products, arithmetic and copies ran while one was open for 0% of the time, Pallas kernels for 39%

profile of v4, /device:TPU:0, one launch (start us, length us, event | category | flops | bytes accessed | tf_op | source)
XLA Modules:
  0.0 61.2 jit_solution(6159135712096530466)
XLA Ops:
  0.0 0.9 %pack.1.near_ref = bf16[1,18432]{1,0:T(2,128)(2,1)S(1)} custom-call(bf16[1,4096]{1,0:T(2,128)(2,1)} %refs_0_.1, bf16[1,14336]{1,0:T(2,128)(2,1)} %refs_1_.2), custom_call_target="tpu_custom_call" | custom-call | tf_op jit(solution)/shard_map/pack/pallas_call | solution.py:316
  0.9 4.1 %collective-permute-start = (bf16[1,18432]{1,0:T(2,128)(2,1)S(1)}, bf16[1,18432]{1,0:T(2,128)(2,1)S(1)}, u32[]{:S(2)}, u32[]{:S(2)}) collective-permute-start(bf16[1,18432]{1,0:T(2,128)(2,1)S(1)} %pack.1.near_ref), channel_id=1, source_target_pairs={{0,8},{1,9},{2,10},{3,11},{4,12},{5,13},{6,14},{7,15},{8,0},{9,1},... | collective-permute-start | bytes 110600 | tf_op jit(solution)/shard_map/ppermute | solution.py:23
  5.0 3.3 %eig_sum.3.after_ref.other_ref.before_ref = f32[8,128]{1,0:T(8,128)S(1)} custom-call(s32[1]{0:T(128)} %bitcast.after_ref.refs_0_, f32[8,128]{1,0:T(8,128)S(1)} %broadcast_in_dim.9.before_ref, f32[896,4096]{1,0:T(8,128)} %refs_5_.3), custom_call_target="tpu_custom_call" | custom-call | flops 917504 | bytes 3670016 | tf_op jit(solution)/shard_map/eig_sum/pallas_call | solution.py:243
  8.3 0.6 collective-permute-done.far_ref.after_ref
  8.9 0.0 copy-start
  8.9 0.0 copy-start.2
  8.9 1.1 %collective-permute-start.1 = (bf16[2,18432]{1,0:T(2,128)(2,1)S(1)}, bf16[2,18432]{1,0:T(2,128)(2,1)S(1)}, u32[]{:S(2)}, u32[]{:S(2)}) collective-permute-start(bf16[2,18432]{1,0:T(2,128)(2,1)S(1)} %join.6.near_ref), channel_id=1, source_target_pairs={{0,4},{1,5},{2,6},{3,7},{4,0},{5,1},{6,2},{7,3},{8,12},{9,13},{10,... | collective-permute-start | bytes 221192 | tf_op jit(solution)/shard_map/ppermute | solution.py:23
  10.0 3.3 %eig_sum.4.before_ref.after_ref.other_ref = f32[8,128]{1,0:T(8,128)S(1)} custom-call(bf16[1,18432]{1,0:T(2,128)(2,1)S(1)} %collective-permute-done.far_ref.after_ref, f32[8,128]{1,0:T(8,128)S(1)} %eig_sum.3.after_ref.other_ref.before_ref, f32[896,4096]{1,0:T(8,128)} %refs_5_.3), custom_call_target="tpu_custom_call" | custom-call | flops 917504 | bytes 3670016 | tf_op jit(solution)/shard_map/eig_sum/pallas_call | solution.py:243
  13.3 0.0 collective-permute-done.1.after_ref.far_ref
  13.4 1.8 %collective-permute-start.2 = (bf16[4,18432]{1,0:T(4,128)(2,1)S(1)}, bf16[4,18432]{1,0:T(4,128)(2,1)S(1)}, u32[]{:S(2)}, u32[]{:S(2)}) collective-permute-start(bf16[4,18432]{1,0:T(4,128)(2,1)S(1)} %join.7.near_ref), channel_id=1, source_target_pairs={{0,2},{1,3},{2,0},{3,1},{4,6},{5,7},{6,4},{7,5},{8,10},{9,11},{10,... | collective-permute-start | bytes 442376 | tf_op jit(solution)/shard_map/ppermute | solution.py:23
  15.2 0.0 copy-done
  15.2 0.0 copy-done.2
  15.2 0.7 %query_in.1.other_ref.refs_4_ = bf16[32,256]{1,0:T(8,128)(2,1)S(1)} custom-call(bf16[2,18432]{1,0:T(2,128)(2,1)S(1)} %collective-permute-done.1.after_ref.far_ref, bf16[32,4096]{1,0:T(8,128)(2,1)S(1)} %copy-done.2, bf16[256,4096]{1,0:T(8,128)(2,1)S(1)} %copy-done), custom_call_target="tpu_custom_call" | custom-call | tf_op jit(solution)/shard_map/query_in/pallas_call | solution.py:331
  15.9 2.2 %eig_sum.5.after_ref.refs_5_ = f32[8,128]{1,0:T(8,128)S(1)} custom-call(bf16[2,18432]{1,0:T(2,128)(2,1)S(1)} %collective-permute-done.1.after_ref.far_ref, f32[8,128]{1,0:T(8,128)S(1)} %eig_sum.4.before_ref.after_ref.other_ref, f32[896,4096]{1,0:T(8,128)} %refs_5_.3), custom_call_target="tpu_custom_call" | custom-call | flops 917504 | bytes 3670016 | tf_op jit(solution)/shard_map/eig_sum/pallas_call | solution.py:243
  18.1 0.5 collective-permute-done.2.far_ref
  18.6 0.1 join.8.refs_1_.refs_0_
  18.7 0.0 copy-start.1
  18.7 0.1 collective-permute-start.3
  18.8 3.0 %load.1.refs_3_ = bf16[896,3584]{1,0:T(8,128)(2,1)S(1)} custom-call(bf16[8,18432]{1,0:T(8,128)(2,1)S(1)} %join.8.refs_1_.refs_0_, bf16[896,14336]{1,0:T(8,128)(2,1)} %refs_4_.5), custom_call_target="tpu_custom_call" | custom-call | bytes 6422528 | tf_op jit(solution)/shard_map/load/pallas_call | solution.py:268
  21.7 0.0 collective-permute-done.3.refs_2_.refs_1_
  21.7 0.8 %train_in.1.refs_0_ = bf16[56,256]{1,0:T(8,128)(2,1)S(1)} custom-call(s32[1]{0:T(128)} %bitcast.after_ref.refs_0_, bf16[8,18432]{1,0:T(8,128)(2,1)S(1)} %join.8.refs_1_.refs_0_, bf16[8,18432]{1,0:T(8,128)(2,1)S(1)} %collective-permute-done.3.refs_2_.refs_1_, bf16[256,4096]{1,0:T(8,128)(2,1)S(1)} %copy-done, bf16[32,256]{1,0:T(8,128)(2,1)S(1)} %query_in.1.other_ref.refs_4_, ...), custom_call_target="tpu_custom_call" | custom-call | tf_op jit(solution)/shard_map/train_in/pallas_call | solution.py:346
  22.5 3.1 %collective-permute-start.4 = (bf16[1,56,256]{2,1,0:T(8,128)(2,1)S(1)}, bf16[1,56,256]{2,1,0:T(8,128)(2,1)S(1)}, u32[]{:S(2)}, u32[]{:S(2)}) collective-permute-start(bf16[1,56,256]{2,1,0:T(8,128)(2,1)S(1)} %bitcast.2), channel_id=1, source_target_pairs={{0,8},{1,9},{2,10},{3,11},{4,12},{5,13},{6,14},{7,15},{8,0},{9,1},... | collective-permute-start | bytes 86024 | tf_op jit(solution)/shard_map/ppermute | solution.py:23
  25.6 0.0 copy-done.1
  25.7 0.1 stack.1.refs_2_.refs_3_
  25.8 3.1 %rotate_out.3 = (f32[896,48]{1,0:T(8,128)S(1)}, bf16[896,3584]{1,0:T(8,128)(2,1)S(1)}) custom-call(bf16[56,256]{1,0:T(8,128)(2,1)S(1)} %train_in.1.refs_0_, f32[896,48]{1,0:T(8,128)S(1)} %broadcast_in_dim.10.refs_1_, bf16[48,14336]{1,0:T(8,128)(2,1)S(1)} %stack.1.refs_2_.refs_3_, bf16[896,3584]{1,0:T(8,128)(2,1)S(1)} %load.1.refs_3_, bf16[896,14336]{1,0:T(8,128)(2,1)} %refs_4_.5), custom_call_target="tpu_custom_call" | custom-call | flops 308281344 | bytes 6422528 | tf_op jit(solution)/shard_map/rotate_out/pallas_call | solution.py:285
  29.0 0.0 collective-permute-done.4.far_ref.refs_0_
  29.0 1.0 %collective-permute-start.5 = (bf16[2,56,256]{2,1,0:T(8,128)(2,1)S(1)}, bf16[2,56,256]{2,1,0:T(8,128)(2,1)S(1)}, u32[]{:S(2)}, u32[]{:S(2)}) collective-permute-start(bf16[2,56,256]{2,1,0:T(8,128)(2,1)S(1)} %join.9.near_ref), channel_id=1, source_target_pairs={{0,4},{1,5},{2,6},{3,7},{4,0},{5,1},{6,2},{7,3},{8,12},{9,13},{10,... | collective-permute-start | bytes 172040 | tf_op jit(solution)/shard_map/ppermute | solution.py:23
  30.0 3.1 %rotate_out.4 = (f32[896,48]{1,0:T(8,128)S(1)}, bf16[896,3584]{1,0:T(8,128)(2,1)S(1)}) custom-call(bf16[1,56,256]{2,1,0:T(8,128)(2,1)S(1)} %collective-permute-done.4.far_ref.refs_0_, f32[896,48]{1,0:T(8,128)S(1)} %get-tuple-element.13.after_ref.other_ref.refs_1_, bf16[48,14336]{1,0:T(8,128)(2,1)S(1)} %stack.1.refs_2_.refs_3_, ...), custom_call_target="tpu_custom_call" | custom-call | flops 308281344 | bytes 6422528 | tf_op jit(solution)/shard_map/rotate_out/pallas_call | solution.py:285
  33.1 0.1 collective-permute-done.5.refs_0_.far_ref
  33.3 1.6 %collective-permute-start.6 = (bf16[4,56,256]{2,1,0:T(8,128)(2,1)S(1)}, bf16[4,56,256]{2,1,0:T(8,128)(2,1)S(1)}, u32[]{:S(2)}, u32[]{:S(2)}) collective-permute-start(bf16[4,56,256]{2,1,0:T(8,128)(2,1)S(1)} %join.10.near_ref), channel_id=1, source_target_pairs={{0,2},{1,3},{2,0},{3,1},{4,6},{5,7},{6,4},{7,5},{8,10},{9,11},{10,... | collective-permute-start | bytes 344072 | tf_op jit(solution)/shard_map/ppermute | solution.py:23
  34.8 3.1 %rotate_out.5 = (f32[896,48]{1,0:T(8,128)S(1)}, bf16[896,3584]{1,0:T(8,128)(2,1)S(1)}) custom-call(bf16[2,56,256]{2,1,0:T(8,128)(2,1)S(1)} %collective-permute-done.5.refs_0_.far_ref, f32[896,48]{1,0:T(8,128)S(1)} %get-tuple-element.15.refs_1_.after_ref.other_ref, bf16[48,14336]{1,0:T(8,128)(2,1)S(1)} %stack.1.refs_2_.refs_3_, ...), custom_call_target="tpu_custom_call" | custom-call | flops 308281344 | bytes 6422528 | tf_op jit(solution)/shard_map/rotate_out/pallas_call | solution.py:285
  38.0 0.2 collective-permute-done.6.far_ref.refs_1_
  38.2 0.1 collective-permute-start.7
  38.2 1.8 %rotate_out_last.1 = (f32[896,48]{1,0:T(8,128)S(1)}, f32[2,896,256]{2,1,0:T(8,128)S(1)}) custom-call(s32[1]{0:T(128)} %bitcast.after_ref.refs_0_, bf16[4,56,256]{2,1,0:T(8,128)(2,1)S(1)} %collective-permute-done.6.far_ref.refs_1_, f32[896,48]{1,0:T(8,128)S(1)} %get-tuple-element.17.after_ref.other_ref.refs_2_, bf16[48,14336]{1,0:T(8,128)(2,1)S(1)} %stack.1.refs_2_.refs_3_, ...), custom_call_target="tpu_custom_call" | custom-call | flops 308281344 | bytes 6422528 | tf_op jit(solution)/shard_map/rotate_out_last/pallas_call | solution.py:295
  40.1 0.0 collective-permute-done.7.refs_2_.refs_4_
  40.1 7.5 %scores.1 = f32[1,512]{1,0:T(1,128)S(1)} custom-call(s32[1]{0:T(128)} %bitcast.after_ref.refs_0_, bf16[8,56,256]{2,1,0:T(8,128)(2,1)S(1)} %join.11.refs_1_.refs_3_, bf16[8,56,256]{2,1,0:T(8,128)(2,1)S(1)} %collective-permute-done.7.refs_2_.refs_4_, bf16[8,56,256]{2,1,0:T(8,128)(2,1)S(1)} %join.11.refs_1_.refs_3_, ...), custom_call_target="tpu_custom_call" | custom-call | tf_op jit(solution)/shard_map/scores/pallas_call | solution.py:379
  47.6 0.1 slice.33
  47.7 0.5 collective-permute-start.8
  48.2 0.1 slice.31
  48.3 0.7 %collective-permute-done.8 = f32[8,32]{1,0:T(8,128)S(1)} collective-permute-done((f32[8,32]{1,0:T(8,128)S(1)}, f32[8,32]{1,0:T(8,128)S(1)}, u32[]{:S(2)}, u32[]{:S(2)}) %collective-permute-start.8) | collective-permute-done | bytes 1056 | tf_op jit(solution)/shard_map/ppermute | solution.py:23
  49.0 1.5 %collective-permute-start.9 = (f32[4,32]{1,0:T(4,128)S(1)}, f32[4,32]{1,0:T(4,128)S(1)}, u32[]{:S(2)}, u32[]{:S(2)}) collective-permute-start(f32[4,32]{1,0:T(4,128)S(1)} %slice.35), channel_id=1, source_target_pairs={{0,2},{1,3},{2,0},{3,1},{4,6},{5,7},{6,4},{7,5},{8,10},{9,11},{10,... | collective-permute-start | bytes 1544 | tf_op jit(solution)/shard_map/ppermute | solution.py:23
  50.5 2.1 %collective-permute-done.9 = f32[4,32]{1,0:T(4,128)S(1)} collective-permute-done((f32[4,32]{1,0:T(4,128)S(1)}, f32[4,32]{1,0:T(4,128)S(1)}, u32[]{:S(2)}, u32[]{:S(2)}) %collective-permute-start.9) | collective-permute-done | bytes 544 | tf_op jit(solution)/shard_map/ppermute | solution.py:23
  52.6 1.1 %collective-permute-start.10 = (f32[2,32]{1,0:T(2,128)S(1)}, f32[2,32]{1,0:T(2,128)S(1)}, u32[]{:S(2)}, u32[]{:S(2)}) collective-permute-start(f32[2,32]{1,0:T(2,128)S(1)} %slice.37), channel_id=1, source_target_pairs={{0,4},{1,5},{2,6},{3,7},{4,0},{5,1},{6,2},{7,3},{8,12},{9,13},{10,... | collective-permute-start | bytes 776 | tf_op jit(solution)/shard_map/ppermute | solution.py:23
  53.7 2.5 %collective-permute-done.10 = f32[2,32]{1,0:T(2,128)S(1)} collective-permute-done((f32[2,32]{1,0:T(2,128)S(1)}, f32[2,32]{1,0:T(2,128)S(1)}, u32[]{:S(2)}, u32[]{:S(2)}) %collective-permute-start.10) | collective-permute-done | bytes 288 | tf_op jit(solution)/shard_map/ppermute | solution.py:23
  56.2 1.8 %collective-permute-start.11 = (f32[1,32]{1,0:T(1,128)S(1)}, f32[1,32]{1,0:T(1,128)S(1)}, u32[]{:S(2)}, u32[]{:S(2)}) collective-permute-start(f32[1,32]{1,0:T(1,128)S(1)} %slice.39), channel_id=1, source_target_pairs={{0,8},{1,9},{2,10},{3,11},{4,12},{5,13},{6,14},{7,15},{8,0},{9,1},... | collective-permute-start | bytes 392 | tf_op jit(solution)/shard_map/ppermute | solution.py:23
  58.0 2.6 %collective-permute-done.11 = f32[1,32]{1,0:T(1,128)S(1)} collective-permute-done((f32[1,32]{1,0:T(1,128)S(1)}, f32[1,32]{1,0:T(1,128)S(1)}, u32[]{:S(2)}, u32[]{:S(2)}) %collective-permute-start.11) | collective-permute-done | bytes 160 | tf_op jit(solution)/shard_map/ppermute | solution.py:23
  60.6 0.5 slice_add_fusion.2
  (14 shorter events, 0.2 us)
Async XLA Ops:
  0.9 8.0 %collective-permute-start = (bf16[1,18432]{1,0:T(2,128)(2,1)S(1)}, bf16[1,18432]{1,0:T(2,128)(2,1)S(1)}, u32[]{:S(2)}, u32[]{:S(2)}) collective-permute-start(bf16[1,18432]{1,0:T(2,128)(2,1)S(1)} %pack.1.near_ref), channel_id=1, source_target_pairs={{0,8},{1,9},{2,10},{3,11},{4,12},{5,13},{6,14},{7,15},{8,0},{9,1},... | collective-permute-start | bytes 110600 | tf_op jit(solution)/shard_map/ppermute | solution.py:23
  8.9 6.3 %copy-start = (bf16[256,4096]{1,0:T(8,128)(2,1)S(1)}, bf16[256,4096]{1,0:T(8,128)(2,1)}, u32[]{:S(2)}) copy-start(bf16[256,4096]{1,0:T(8,128)(2,1)} %refs_3_.1) | copy-start | bytes 6291460
  8.9 6.3 %copy-start.2 = (bf16[32,4096]{1,0:T(8,128)(2,1)S(1)}, bf16[32,4096]{1,0:T(8,128)(2,1)}, u32[]{:S(2)}) copy-start(bf16[32,4096]{1,0:T(8,128)(2,1)} %query_ref.1) | copy-start | bytes 786436
  8.9 4.4 %collective-permute-start.1 = (bf16[2,18432]{1,0:T(2,128)(2,1)S(1)}, bf16[2,18432]{1,0:T(2,128)(2,1)S(1)}, u32[]{:S(2)}, u32[]{:S(2)}) collective-permute-start(bf16[2,18432]{1,0:T(2,128)(2,1)S(1)} %join.6.near_ref), channel_id=1, source_target_pairs={{0,4},{1,5},{2,6},{3,7},{4,0},{5,1},{6,2},{7,3},{8,12},{9,13},{10,... | collective-permute-start | bytes 221192 | tf_op jit(solution)/shard_map/ppermute | solution.py:23
  13.4 5.2 %collective-permute-start.2 = (bf16[4,18432]{1,0:T(4,128)(2,1)S(1)}, bf16[4,18432]{1,0:T(4,128)(2,1)S(1)}, u32[]{:S(2)}, u32[]{:S(2)}) collective-permute-start(bf16[4,18432]{1,0:T(4,128)(2,1)S(1)} %join.7.near_ref), channel_id=1, source_target_pairs={{0,2},{1,3},{2,0},{3,1},{4,6},{5,7},{6,4},{7,5},{8,10},{9,11},{10,... | collective-permute-start | bytes 442376 | tf_op jit(solution)/shard_map/ppermute | solution.py:23
  18.7 7.0 %copy-start.1 = (bf16[32,14336]{1,0:T(8,128)(2,1)S(1)}, bf16[32,14336]{1,0:T(8,128)(2,1)}, u32[]{:S(2)}) copy-start(bf16[32,14336]{1,0:T(8,128)(2,1)} %refs_2_.1) | copy-start | bytes 2752516
  18.7 3.0 %collective-permute-start.3 = (bf16[8,18432]{1,0:T(8,128)(2,1)S(1)}, bf16[8,18432]{1,0:T(8,128)(2,1)S(1)}, u32[]{:S(2)}, u32[]{:S(2)}) collective-permute-start(bf16[8,18432]{1,0:T(8,128)(2,1)S(1)} %join.8.refs_1_.refs_0_), channel_id=1, source_target_pairs={{0,1},{1,0},{2,3},{3,2},{4,5},{5,4},{6,7},{7,6},{8,9},{9,8},{10,11... | collective-permute-start | bytes 884744 | tf_op jit(solution)/shard_map/ppermute | solution.py:23
  22.5 6.4 %collective-permute-start.4 = (bf16[1,56,256]{2,1,0:T(8,128)(2,1)S(1)}, bf16[1,56,256]{2,1,0:T(8,128)(2,1)S(1)}, u32[]{:S(2)}, u32[]{:S(2)}) collective-permute-start(bf16[1,56,256]{2,1,0:T(8,128)(2,1)S(1)} %bitcast.2), channel_id=1, source_target_pairs={{0,8},{1,9},{2,10},{3,11},{4,12},{5,13},{6,14},{7,15},{8,0},{9,1},... | collective-permute-start | bytes 86024 | tf_op jit(solution)/shard_map/ppermute | solution.py:23
  29.0 4.2 %collective-permute-start.5 = (bf16[2,56,256]{2,1,0:T(8,128)(2,1)S(1)}, bf16[2,56,256]{2,1,0:T(8,128)(2,1)S(1)}, u32[]{:S(2)}, u32[]{:S(2)}) collective-permute-start(bf16[2,56,256]{2,1,0:T(8,128)(2,1)S(1)} %join.9.near_ref), channel_id=1, source_target_pairs={{0,4},{1,5},{2,6},{3,7},{4,0},{5,1},{6,2},{7,3},{8,12},{9,13},{10,... | collective-permute-start | bytes 172040 | tf_op jit(solution)/shard_map/ppermute | solution.py:23
  33.3 4.9 %collective-permute-start.6 = (bf16[4,56,256]{2,1,0:T(8,128)(2,1)S(1)}, bf16[4,56,256]{2,1,0:T(8,128)(2,1)S(1)}, u32[]{:S(2)}, u32[]{:S(2)}) collective-permute-start(bf16[4,56,256]{2,1,0:T(8,128)(2,1)S(1)} %join.10.near_ref), channel_id=1, source_target_pairs={{0,2},{1,3},{2,0},{3,1},{4,6},{5,7},{6,4},{7,5},{8,10},{9,11},{10,... | collective-permute-start | bytes 344072 | tf_op jit(solution)/shard_map/ppermute | solution.py:23
  38.2 1.9 %collective-permute-start.7 = (bf16[8,56,256]{2,1,0:T(8,128)(2,1)S(1)}, bf16[8,56,256]{2,1,0:T(8,128)(2,1)S(1)}, u32[]{:S(2)}, u32[]{:S(2)}) collective-permute-start(bf16[8,56,256]{2,1,0:T(8,128)(2,1)S(1)} %join.11.refs_1_.refs_3_), channel_id=1, source_target_pairs={{0,1},{1,0},{2,3},{3,2},{4,5},{5,4},{6,7},{7,6},{8,9},{9,8},{10,11... | collective-permute-start | bytes 688136 | tf_op jit(solution)/shard_map/ppermute | solution.py:23
  47.7 1.3 %collective-permute-start.8 = (f32[8,32]{1,0:T(8,128)S(1)}, f32[8,32]{1,0:T(8,128)S(1)}, u32[]{:S(2)}, u32[]{:S(2)}) collective-permute-start(f32[8,32]{1,0:T(8,128)S(1)} %slice.33), channel_id=1, source_target_pairs={{0,1},{1,0},{2,3},{3,2},{4,5},{5,4},{6,7},{7,6},{8,9},{9,8},{10,11... | collective-permute-start | bytes 3080 | tf_op jit(solution)/shard_map/ppermute | solution.py:23
  49.0 3.6 %collective-permute-start.9 = (f32[4,32]{1,0:T(4,128)S(1)}, f32[4,32]{1,0:T(4,128)S(1)}, u32[]{:S(2)}, u32[]{:S(2)}) collective-permute-start(f32[4,32]{1,0:T(4,128)S(1)} %slice.35), channel_id=1, source_target_pairs={{0,2},{1,3},{2,0},{3,1},{4,6},{5,7},{6,4},{7,5},{8,10},{9,11},{10,... | collective-permute-start | bytes 1544 | tf_op jit(solution)/shard_map/ppermute | solution.py:23
  52.6 3.6 %collective-permute-start.10 = (f32[2,32]{1,0:T(2,128)S(1)}, f32[2,32]{1,0:T(2,128)S(1)}, u32[]{:S(2)}, u32[]{:S(2)}) collective-permute-start(f32[2,32]{1,0:T(2,128)S(1)} %slice.37), channel_id=1, source_target_pairs={{0,4},{1,5},{2,6},{3,7},{4,0},{5,1},{6,2},{7,3},{8,12},{9,13},{10,... | collective-permute-start | bytes 776 | tf_op jit(solution)/shard_map/ppermute | solution.py:23
  56.2 4.4 %collective-permute-start.11 = (f32[1,32]{1,0:T(1,128)S(1)}, f32[1,32]{1,0:T(1,128)S(1)}, u32[]{:S(2)}, u32[]{:S(2)}) collective-permute-start(f32[1,32]{1,0:T(1,128)S(1)} %slice.39), channel_id=1, source_target_pairs={{0,8},{1,9},{2,10},{3,11},{4,12},{5,13},{6,14},{7,15},{8,0},{9,1},... | collective-permute-start | bytes 392 | tf_op jit(solution)/shard_map/ppermute | solution.py:23
